TPU v7x, 128 devices: a whole 4x4x4 slice. The times are simulated.
128 devices in a mesh: lat: 4 (over z_lo, core), lon: 32 (over y, z_hi, x).
Axes of the slice: x: 4, y: 4, z: 4 (z_hi: 2, z_lo: 2; z = z_hi * 2 + z_lo), core: 2. Of those that a mesh axis runs over, the one named last changes fastest.
Arguments:
- latent: bfloat16 [4, 384, 384, 512], P(None, 'lat', 'lon'), may hold values from -6 to 6
- attention_gain: float32 [512], replicated, may hold values from 0.25 to 1.75
- triple_weight: bfloat16 [512, 1536], replicated, may hold values from -0.25 to 0.25
- head_scale: float32 [8], replicated, may hold values from 0.5 to 64, as said below
- output_weight: bfloat16 [512, 512], replicated, may hold values from -0.25 to 0.25
- feed_gain: float32 [512], replicated, may hold values from 0.25 to 1.75
- up_weight: bfloat16 [512, 2048], replicated, may hold values from -0.25 to 0.25
- down_weight: bfloat16 [2048, 512], replicated, may hold values from -0.125 to 0.125
Outputs:
- block_out: bfloat16 [4, 384, 384, 512], P(None, 'lat', 'lon')
Inputs may be any that keep to these rules, and one draw needn't show every extreme that they name: `head_scale`: positive factor for each head.
All inputs are finite; a program needn't handle non-finite values.
Results may differ from a plain program's by a relative error of at most 0.0065.
The roundings to bfloat16 on the way count: a program that leaves them out, or rounds other values in their place, can miss the bound.
Values may be sent and summed in bfloat16 or wider, within the bound.
No kernel may reach another device: no remote copies, remote signals or barrier semaphores. Data moves between devices by JAX's collectives and lax.ppermute only.
A program may use at most 256 MiB of HBM per device.

v0:
```python
import jax
import jax.numpy as jnp
from jax import lax
from jax.sharding import PartitionSpec as P

WL = 2
WLAT = 6
WLON = 12


epsilon = 1e-05


def from_behind(shard, axis, by):
    count = lax.axis_size(axis)
    return lax.ppermute(shard, axis, [(i, (i + by) % count) for i in range(count)])


def layer_norm(values, scaling):
    average = jnp.mean(values, axis=-1, keepdims=True)
    centred = values - average
    spread = jnp.mean(centred * centred, axis=-1, keepdims=True)
    return centred * lax.rsqrt(spread + epsilon) * scaling


def attend(shifted, start_row, total_rows, triple_weight, head_scale):
    levels, tile_rows, tile_cols, channels = shifted.shape
    heads = head_scale.shape[0]
    head_dim = channels // heads
    level_wins = levels // WL
    row_wins = tile_rows // WLAT
    col_wins = tile_cols // WLON
    window_len = WL * WLAT * WLON
    projected = jnp.dot(
        shifted.reshape(-1, channels), triple_weight, preferred_element_type=jnp.float32
    )
    projected = projected.astype(jnp.bfloat16).reshape(levels, tile_rows, tile_cols, 3 * channels)
    factor = head_scale / jnp.sqrt(jnp.float32(head_dim))

    def one_band(band_index, outcome):
        band_start = band_index * WLAT
        band = lax.dynamic_slice_in_dim(projected, band_start, WLAT, 1)
        band = band.reshape(level_wins, WL, WLAT, col_wins, WLON, 3, heads, head_dim)
        queries = band[:, :, :, :, :, 0]
        keys_part = band[:, :, :, :, :, 1]
        values_part = band[:, :, :, :, :, 2]
        scores = jnp.einsum(
            "alrechd,amsefhd->aehlrcmsf", queries, keys_part, preferred_element_type=jnp.float32
        )
        scores = scores.reshape(level_wins, col_wins, heads, window_len, window_len)
        scores = scores * factor[None, None, :, None, None]
        row_ids = (start_row + band_start + jnp.arange(WLAT, dtype=jnp.int32)) % total_rows
        token_flag = jnp.broadcast_to(
            (row_ids < WLAT // 2).reshape(1, WLAT, 1), (WL, WLAT, WLON)
        ).reshape(window_len)
        allowed = token_flag[:, None] == token_flag[None, :]
        scores = jnp.where(allowed[None, None, None], scores, -1e30)
        row_max = jnp.max(scores, axis=-1, keepdims=True)
        weights = jnp.exp(scores - row_max)
        attn_probs = (weights / jnp.sum(weights, axis=-1, keepdims=True)).astype(jnp.bfloat16)
        attn_probs = attn_probs.reshape(level_wins, col_wins, heads, WL, WLAT, WLON, WL, WLAT, WLON)
        mixed = jnp.einsum(
            "aehlrcmsf,amsefhd->alrechd",
            attn_probs,
            values_part,
            preferred_element_type=jnp.float32,
        )
        mixed = mixed.astype(jnp.bfloat16).reshape(levels, WLAT, tile_cols, channels)
        return lax.dynamic_update_slice_in_dim(outcome, mixed, band_start, 1)

    initial = jnp.zeros((levels, tile_rows, tile_cols, channels), jnp.bfloat16)
    return lax.fori_loop(0, row_wins, one_band, initial)


def per_device(
    latent,
    attention_gain,
    triple_weight,
    head_scale,
    output_weight,
    feed_gain,
    up_weight,
    down_weight,
):
    levels, tile_rows, tile_cols, channels = latent.shape
    total_rows = tile_rows * lax.axis_size("lat")
    first_row = lax.axis_index("lat") * tile_rows
    half_lat = WLAT // 2
    half_lon = WLON // 2
    normed = layer_norm(latent.astype(jnp.float32), attention_gain).astype(jnp.bfloat16)
    from_right = from_behind(normed[:, :, :half_lon], "lon", -1)
    widened = jnp.concatenate([normed[:, :, half_lon:], from_right], axis=2)
    from_below = from_behind(widened[:, :half_lat], "lat", -1)
    shifted = jnp.concatenate([widened[:, half_lat:], from_below], axis=1)
    attended = attend(shifted, first_row + half_lat, total_rows, triple_weight, head_scale)
    from_above = from_behind(attended[:, tile_rows - half_lat :], "lat", 1)
    restored = jnp.concatenate([from_above, attended[:, : tile_rows - half_lat]], axis=1)
    from_left = from_behind(restored[:, :, tile_cols - half_lon :], "lon", 1)
    attended = jnp.concatenate([from_left, restored[:, :, : tile_cols - half_lon]], axis=2)
    inputs = latent.reshape(-1, channels)
    residual = inputs.astype(jnp.float32) + jnp.dot(
        attended.reshape(-1, channels), output_weight, preferred_element_type=jnp.float32
    )
    feed_normed = layer_norm(residual, feed_gain).astype(jnp.bfloat16)
    hidden = jnp.dot(feed_normed, up_weight, preferred_element_type=jnp.float32)
    activated = jax.nn.gelu(hidden, approximate=False).astype(jnp.bfloat16)
    block_out = residual + jnp.dot(activated, down_weight, preferred_element_type=jnp.float32)
    return block_out.astype(jnp.bfloat16).reshape(levels, tile_rows, tile_cols, channels)


def solution(mesh):
    in_specs = (P(None, "lat", "lon", None), P(), P(), P(), P(), P(), P(), P())
    out_specs = P(None, "lat", "lon", None)
    return jax.shard_map(
        per_device, mesh=mesh, in_specs=in_specs, out_specs=out_specs, check_vma=False
    )
```

profile of v0, /device:TPU:1, one launch (start us, length us, event | category | flops | bytes accessed | tf_op | source)
XLA Modules:
  0.0 997.8 jit_solution(8139945189493066248)
XLA Ops:
  13.9 9.1 collective-permute-start
  23.0 50.2 %collective-permute-done = bf16[4,96,6,512]{3,1,2,0:T(8,128)(2,1)} collective-permute-done((bf16[4,96,6,512]{3,1,2,0:T(8,128)(2,1)}, bf16[4,96,6,512]{3,1,2,0:T(8,128)(2,1)}, u32[]{:S(2)}, u32[]{:S(2)}) %collective-permute-start) | collective-permute-done | bytes 2359328 | tf_op jit(solution)/shard_map/ppermute | solution.py:16
  86.1 8.6 reshape.208
  94.7 12.7 %convolution_convert_fusion = bf16[4608,1536]{1,0:T(8,128)(2,1)} fusion(bf16[4608,512]{1,0:T(8,128)(2,1)} %reshape.208, bf16[512,1536]{1,0:T(8,128)(2,1)} %param.12), kind=kOutput, calls=%fused_computation.37 | convolution fusion | flops 7254835200 | bytes 20447232 | tf_op jit(solution)/shard_map/dot_general | solution.py:34
  107.4 21.3 %reshape.209 = bf16[4,96,12,1536]{3,2,1,0:T(8,128)(2,1)} reshape(bf16[4608,1536]{1,0:T(8,128)(2,1)} %convolution_convert_fusion) | data formatting | bytes 28311552 | tf_op jit(solution)/shard_map/reshape | solution.py:37
  128.7 17.6 %copy.19 = bf16[4,96,12,1536]{3,0,2,1:T(4,128)(2,1)} copy(bf16[4,96,12,1536]{3,2,1,0:T(8,128)(2,1)} %reshape.209) | data formatting | bytes 28311552 | tf_op jit(solution)/shard_map/while | solution.py:72
  150.9 618.2 %while.15 = (s32[]{:T(128)}, bf16[4,96,12,512]{3,0,2,1:T(4,128)(2,1)}, bf16[4,96,12,1536]{3,0,2,1:T(4,128)(2,1)}, s32[]{:T(128)}, f32[8]{0:T(128)S(1)}, /*index=5*/s32[]{:T(128)}, s32[]{:T(128)}, s32[]{:T(128)}, s32[]{:T(128)}) while((s32[]{:T(128)}, bf16[4,96,12,512]{3,0,2,1:T(4,128)(2,1)}, bf16[4,96,12,1536]{3,0,2,1:T(4,128)(2,1)}, ...), condition=%wide.region_5.6_spmd, body=%wide.region_2.5_spmd.sunk | while | flops 89079608 | bytes 12368143 | solution.py:72
  156.5 9.3 fusion.85
  165.8 12.8 %fusion.86 = f32[2,8,2,6,12]{4,3,2,1,0:T(8,128)S(1)} fusion(f32[2,8,2,6,12,2,6,12]{4,7,6,5,3,2,1,0:T(8,128)} %get-tuple-element.201, f32[2,8,2,6,12]{4,3,2,1,0:T(8,128)S(1)} %get-tuple-element.202, f32[8]{0:T(128)S(1)} %get-tuple-element.226, pred[2,6,12,2,6,12]{2,5,4,3,1,0:T(8,128)(4,1)S(1)} %broadcast_compare_fusion.2), kind=kLoop, calls=%fused_computation.4.clone.1 | loop fusion | flops 1324800 | bytes 1366304 | tf_op jit(solution)/shard_map/while/body/eval_jaxpr/reduce_sum | solution.py:60
  178.6 9.8 fusion.87
  195.1 9.3 fusion.85
  204.4 12.8 %fusion.86 = f32[2,8,2,6,12]{4,3,2,1,0:T(8,128)S(1)} fusion(f32[2,8,2,6,12,2,6,12]{4,7,6,5,3,2,1,0:T(8,128)} %get-tuple-element.201, f32[2,8,2,6,12]{4,3,2,1,0:T(8,128)S(1)} %get-tuple-element.202, f32[8]{0:T(128)S(1)} %get-tuple-element.226, pred[2,6,12,2,6,12]{2,5,4,3,1,0:T(8,128)(4,1)S(1)} %broadcast_compare_fusion.2), kind=kLoop, calls=%fused_computation.4.clone.1 | loop fusion | flops 1324800 | bytes 1366304 | tf_op jit(solution)/shard_map/while/body/eval_jaxpr/reduce_sum | solution.py:60
  217.2 9.8 fusion.87
  233.7 9.3 fusion.85
  243.0 12.8 %fusion.86 = f32[2,8,2,6,12]{4,3,2,1,0:T(8,128)S(1)} fusion(f32[2,8,2,6,12,2,6,12]{4,7,6,5,3,2,1,0:T(8,128)} %get-tuple-element.201, f32[2,8,2,6,12]{4,3,2,1,0:T(8,128)S(1)} %get-tuple-element.202, f32[8]{0:T(128)S(1)} %get-tuple-element.226, pred[2,6,12,2,6,12]{2,5,4,3,1,0:T(8,128)(4,1)S(1)} %broadcast_compare_fusion.2), kind=kLoop, calls=%fused_computation.4.clone.1 | loop fusion | flops 1324800 | bytes 1366304 | tf_op jit(solution)/shard_map/while/body/eval_jaxpr/reduce_sum | solution.py:60
  255.8 9.8 fusion.87
  272.3 9.3 fusion.85
  281.6 12.8 %fusion.86 = f32[2,8,2,6,12]{4,3,2,1,0:T(8,128)S(1)} fusion(f32[2,8,2,6,12,2,6,12]{4,7,6,5,3,2,1,0:T(8,128)} %get-tuple-element.201, f32[2,8,2,6,12]{4,3,2,1,0:T(8,128)S(1)} %get-tuple-element.202, f32[8]{0:T(128)S(1)} %get-tuple-element.226, pred[2,6,12,2,6,12]{2,5,4,3,1,0:T(8,128)(4,1)S(1)} %broadcast_compare_fusion.2), kind=kLoop, calls=%fused_computation.4.clone.1 | loop fusion | flops 1324800 | bytes 1366304 | tf_op jit(solution)/shard_map/while/body/eval_jaxpr/reduce_sum | solution.py:60
  294.4 9.8 fusion.87
  310.9 9.3 fusion.85
  320.2 12.8 %fusion.86 = f32[2,8,2,6,12]{4,3,2,1,0:T(8,128)S(1)} fusion(f32[2,8,2,6,12,2,6,12]{4,7,6,5,3,2,1,0:T(8,128)} %get-tuple-element.201, f32[2,8,2,6,12]{4,3,2,1,0:T(8,128)S(1)} %get-tuple-element.202, f32[8]{0:T(128)S(1)} %get-tuple-element.226, pred[2,6,12,2,6,12]{2,5,4,3,1,0:T(8,128)(4,1)S(1)} %broadcast_compare_fusion.2), kind=kLoop, calls=%fused_computation.4.clone.1 | loop fusion | flops 1324800 | bytes 1366304 | tf_op jit(solution)/shard_map/while/body/eval_jaxpr/reduce_sum | solution.py:60
  333.0 9.8 fusion.87
  349.5 9.3 fusion.85
  358.8 12.8 %fusion.86 = f32[2,8,2,6,12]{4,3,2,1,0:T(8,128)S(1)} fusion(f32[2,8,2,6,12,2,6,12]{4,7,6,5,3,2,1,0:T(8,128)} %get-tuple-element.201, f32[2,8,2,6,12]{4,3,2,1,0:T(8,128)S(1)} %get-tuple-element.202, f32[8]{0:T(128)S(1)} %get-tuple-element.226, pred[2,6,12,2,6,12]{2,5,4,3,1,0:T(8,128)(4,1)S(1)} %broadcast_compare_fusion.2), kind=kLoop, calls=%fused_computation.4.clone.1 | loop fusion | flops 1324800 | bytes 1366304 | tf_op jit(solution)/shard_map/while/body/eval_jaxpr/reduce_sum | solution.py:60
  371.6 9.8 fusion.87
  388.1 9.3 fusion.85
  397.4 12.8 %fusion.86 = f32[2,8,2,6,12]{4,3,2,1,0:T(8,128)S(1)} fusion(f32[2,8,2,6,12,2,6,12]{4,7,6,5,3,2,1,0:T(8,128)} %get-tuple-element.201, f32[2,8,2,6,12]{4,3,2,1,0:T(8,128)S(1)} %get-tuple-element.202, f32[8]{0:T(128)S(1)} %get-tuple-element.226, pred[2,6,12,2,6,12]{2,5,4,3,1,0:T(8,128)(4,1)S(1)} %broadcast_compare_fusion.2), kind=kLoop, calls=%fused_computation.4.clone.1 | loop fusion | flops 1324800 | bytes 1366304 | tf_op jit(solution)/shard_map/while/body/eval_jaxpr/reduce_sum | solution.py:60
  410.2 9.8 fusion.87
  426.7 9.3 fusion.85
  436.0 12.8 %fusion.86 = f32[2,8,2,6,12]{4,3,2,1,0:T(8,128)S(1)} fusion(f32[2,8,2,6,12,2,6,12]{4,7,6,5,3,2,1,0:T(8,128)} %get-tuple-element.201, f32[2,8,2,6,12]{4,3,2,1,0:T(8,128)S(1)} %get-tuple-element.202, f32[8]{0:T(128)S(1)} %get-tuple-element.226, pred[2,6,12,2,6,12]{2,5,4,3,1,0:T(8,128)(4,1)S(1)} %broadcast_compare_fusion.2), kind=kLoop, calls=%fused_computation.4.clone.1 | loop fusion | flops 1324800 | bytes 1366304 | tf_op jit(solution)/shard_map/while/body/eval_jaxpr/reduce_sum | solution.py:60
  448.8 9.8 fusion.87
  465.3 9.3 fusion.85
  474.6 12.8 %fusion.86 = f32[2,8,2,6,12]{4,3,2,1,0:T(8,128)S(1)} fusion(f32[2,8,2,6,12,2,6,12]{4,7,6,5,3,2,1,0:T(8,128)} %get-tuple-element.201, f32[2,8,2,6,12]{4,3,2,1,0:T(8,128)S(1)} %get-tuple-element.202, f32[8]{0:T(128)S(1)} %get-tuple-element.226, pred[2,6,12,2,6,12]{2,5,4,3,1,0:T(8,128)(4,1)S(1)} %broadcast_compare_fusion.2), kind=kLoop, calls=%fused_computation.4.clone.1 | loop fusion | flops 1324800 | bytes 1366304 | tf_op jit(solution)/shard_map/while/body/eval_jaxpr/reduce_sum | solution.py:60
  487.4 9.8 fusion.87
  503.9 9.3 fusion.85
  513.2 12.8 %fusion.86 = f32[2,8,2,6,12]{4,3,2,1,0:T(8,128)S(1)} fusion(f32[2,8,2,6,12,2,6,12]{4,7,6,5,3,2,1,0:T(8,128)} %get-tuple-element.201, f32[2,8,2,6,12]{4,3,2,1,0:T(8,128)S(1)} %get-tuple-element.202, f32[8]{0:T(128)S(1)} %get-tuple-element.226, pred[2,6,12,2,6,12]{2,5,4,3,1,0:T(8,128)(4,1)S(1)} %broadcast_compare_fusion.2), kind=kLoop, calls=%fused_computation.4.clone.1 | loop fusion | flops 1324800 | bytes 1366304 | tf_op jit(solution)/shard_map/while/body/eval_jaxpr/reduce_sum | solution.py:60
  526.0 9.8 fusion.87
  542.5 9.3 fusion.85
  551.8 12.8 %fusion.86 = f32[2,8,2,6,12]{4,3,2,1,0:T(8,128)S(1)} fusion(f32[2,8,2,6,12,2,6,12]{4,7,6,5,3,2,1,0:T(8,128)} %get-tuple-element.201, f32[2,8,2,6,12]{4,3,2,1,0:T(8,128)S(1)} %get-tuple-element.202, f32[8]{0:T(128)S(1)} %get-tuple-element.226, pred[2,6,12,2,6,12]{2,5,4,3,1,0:T(8,128)(4,1)S(1)} %broadcast_compare_fusion.2), kind=kLoop, calls=%fused_computation.4.clone.1 | loop fusion | flops 1324800 | bytes 1366304 | tf_op jit(solution)/shard_map/while/body/eval_jaxpr/reduce_sum | solution.py:60
  564.6 9.8 fusion.87
  581.1 9.3 fusion.85
  590.4 12.8 %fusion.86 = f32[2,8,2,6,12]{4,3,2,1,0:T(8,128)S(1)} fusion(f32[2,8,2,6,12,2,6,12]{4,7,6,5,3,2,1,0:T(8,128)} %get-tuple-element.201, f32[2,8,2,6,12]{4,3,2,1,0:T(8,128)S(1)} %get-tuple-element.202, f32[8]{0:T(128)S(1)} %get-tuple-element.226, pred[2,6,12,2,6,12]{2,5,4,3,1,0:T(8,128)(4,1)S(1)} %broadcast_compare_fusion.2), kind=kLoop, calls=%fused_computation.4.clone.1 | loop fusion | flops 1324800 | bytes 1366304 | tf_op jit(solution)/shard_map/while/body/eval_jaxpr/reduce_sum | solution.py:60
  603.2 9.8 fusion.87
  619.7 9.3 fusion.85
  629.0 12.8 %fusion.86 = f32[2,8,2,6,12]{4,3,2,1,0:T(8,128)S(1)} fusion(f32[2,8,2,6,12,2,6,12]{4,7,6,5,3,2,1,0:T(8,128)} %get-tuple-element.201, f32[2,8,2,6,12]{4,3,2,1,0:T(8,128)S(1)} %get-tuple-element.202, f32[8]{0:T(128)S(1)} %get-tuple-element.226, pred[2,6,12,2,6,12]{2,5,4,3,1,0:T(8,128)(4,1)S(1)} %broadcast_compare_fusion.2), kind=kLoop, calls=%fused_computation.4.clone.1 | loop fusion | flops 1324800 | bytes 1366304 | tf_op jit(solution)/shard_map/while/body/eval_jaxpr/reduce_sum | solution.py:60
  641.8 9.8 fusion.87
  658.3 9.3 fusion.85
  667.6 12.8 %fusion.86 = f32[2,8,2,6,12]{4,3,2,1,0:T(8,128)S(1)} fusion(f32[2,8,2,6,12,2,6,12]{4,7,6,5,3,2,1,0:T(8,128)} %get-tuple-element.201, f32[2,8,2,6,12]{4,3,2,1,0:T(8,128)S(1)} %get-tuple-element.202, f32[8]{0:T(128)S(1)} %get-tuple-element.226, pred[2,6,12,2,6,12]{2,5,4,3,1,0:T(8,128)(4,1)S(1)} %broadcast_compare_fusion.2), kind=kLoop, calls=%fused_computation.4.clone.1 | loop fusion | flops 1324800 | bytes 1366304 | tf_op jit(solution)/shard_map/while/body/eval_jaxpr/reduce_sum | solution.py:60
  680.4 9.8 fusion.87
  696.9 9.3 fusion.85
  706.2 12.8 %fusion.86 = f32[2,8,2,6,12]{4,3,2,1,0:T(8,128)S(1)} fusion(f32[2,8,2,6,12,2,6,12]{4,7,6,5,3,2,1,0:T(8,128)} %get-tuple-element.201, f32[2,8,2,6,12]{4,3,2,1,0:T(8,128)S(1)} %get-tuple-element.202, f32[8]{0:T(128)S(1)} %get-tuple-element.226, pred[2,6,12,2,6,12]{2,5,4,3,1,0:T(8,128)(4,1)S(1)} %broadcast_compare_fusion.2), kind=kLoop, calls=%fused_computation.4.clone.1 | loop fusion | flops 1324800 | bytes 1366304 | tf_op jit(solution)/shard_map/while/body/eval_jaxpr/reduce_sum | solution.py:60
  719.0 9.8 fusion.87
  735.5 9.3 fusion.85
  744.8 12.8 %fusion.86 = f32[2,8,2,6,12]{4,3,2,1,0:T(8,128)S(1)} fusion(f32[2,8,2,6,12,2,6,12]{4,7,6,5,3,2,1,0:T(8,128)} %get-tuple-element.201, f32[2,8,2,6,12]{4,3,2,1,0:T(8,128)S(1)} %get-tuple-element.202, f32[8]{0:T(128)S(1)} %get-tuple-element.226, pred[2,6,12,2,6,12]{2,5,4,3,1,0:T(8,128)(4,1)S(1)} %broadcast_compare_fusion.2), kind=kLoop, calls=%fused_computation.4.clone.1 | loop fusion | flops 1324800 | bytes 1366304 | tf_op jit(solution)/shard_map/while/body/eval_jaxpr/reduce_sum | solution.py:60
  757.6 9.8 fusion.87
  779.7 7.5 copy.17
  787.2 11.7 %reshape.212 = f32[4608,512]{1,0:T(8,128)} reshape(f32[4,96,12,512]{3,2,1,0:T(8,128)} %copy.17) | data formatting | bytes 18874368 | tf_op jit(solution)/shard_map/convert_element_type | solution.py:101
  799.0 41.0 %collective-permute-done.3 = bf16[4,96,6,512]{3,0,2,1:T(4,128)(2,1)} collective-permute-done((bf16[4,96,6,512]{3,0,2,1:T(4,128)(2,1)}, bf16[4,96,6,512]{3,0,2,1:T(4,128)(2,1)}, u32[]{:S(2)}, u32[]{:S(2)}) %collective-permute-start.3) | collective-permute-done | bytes 2359328 | tf_op jit(solution)/shard_map/ppermute | solution.py:16
  849.1 8.6 reshape.210
  857.7 13.5 %fusion.63 = (f32[4608]{0:T(1024)S(1)}, f32[4608,512]{1,0:T(8,128)S(1)}) fusion(f32[4608,512]{1,0:T(8,128)} %reshape.212, bf16[4608,512]{1,0:T(8,128)(2,1)} %reshape.210, bf16[512,512]{1,0:T(8,128)(2,1)S(1)} %copy-done.3), kind=kOutput, calls=%fused_computation.95 | convolution fusion | flops 2420633088 | bytes 24135680 | tf_op jit(solution)/shard_map/dot_general | solution.py:101
  874.2 91.7 %fusion.76 = bf16[4608,2048]{1,0:T(8,128)(2,1)} fusion(bf16[512,2048]{1,0:T(8,128)(2,1)S(1)} %copy-done, f32[4608,512]{1,0:T(8,128)S(1)} %get-tuple-element.162, f32[512]{0:T(512)S(1)} %copy-done.5, f32[4608]{0:T(1024)S(1)} %add_rsqrt_fusion.1, f32[4608]{0:T(1024)S(1)} %broadcast_multiply_fusion.1), kind=kOutput, calls=%fused_computation.21.clone.clone.clone.clone.1 | convolution fusion | flops 10286530560 | bytes 30447616 | tf_op jit(solution)/shard_map/dot_general | solution.py:105
  966.0 15.5 %add_convert_fusion = bf16[4608,512]{1,0:T(8,128)(2,1)} fusion(f32[4608,512]{1,0:T(8,128)S(1)} %get-tuple-element.162, bf16[2048,512]{1,0:T(8,128)(2,1)S(1)} %copy-done.4, bf16[4608,2048]{1,0:T(8,128)(2,1)} %fusion.76), kind=kOutput, calls=%fused_computation.40 | convolution fusion | flops 9668395008 | bytes 35127296 | tf_op jit(solution)/shard_map/dot_general | solution.py:107
  981.5 8.4 reshape.211
  989.9 7.6 copy.21
  (172 shorter events, 161.9 us)
Async XLA Ops:
  0.0 874.2 %copy-start = (bf16[512,2048]{1,0:T(8,128)(2,1)S(1)}, bf16[512,2048]{1,0:T(8,128)(2,1)}, u32[]{:S(2)}) copy-start(bf16[512,2048]{1,0:T(8,128)(2,1)} %param.16) | copy-start | bytes 6291460
  0.0 22.9 %copy-start.6 = (f32[8]{0:T(128)S(1)}, f32[8]{0:T(128)}, u32[]{:S(2)}) copy-start(f32[8]{0:T(128)} %param.13) | copy-start | bytes 100
  13.9 59.3 %collective-permute-start = (bf16[4,96,6,512]{3,1,2,0:T(8,128)(2,1)}, bf16[4,96,6,512]{3,1,2,0:T(8,128)(2,1)}, u32[]{:S(2)}, u32[]{:S(2)}) collective-permute-start(bf16[4,96,6,512]{3,1,2,0:T(8,128)(2,1)} %get-tuple-element.160), channel_id=1, source_target_pairs={{0,31},{1,0},{2,1},{3,2},{4,3},{5,4},{6,5},{7,6},{8,7},{9,8},{10,9... | collective-permute-start | bytes 7077896 | tf_op jit(solution)/shard_map/ppermute | solution.py:16
  74.3 5.8 collective-permute-start.1
  769.1 10.6 %slice-start = ((s8[4718592]{0:T(1024)(128)(4,1)}), s8[4194304]{0:T(1024)(128)(4,1)S(1)}, s32[]{:S(2)}) async-start(s8[4718592]{0:T(1024)(128)(4,1)} %bitcast.62), calls=%async_computation | async-start | bytes 8388608
  770.2 9.5 slice-start.1
  770.2 4.8 collective-permute-start.2
  774.9 2.1 copy-start.2
  779.7 60.3 %collective-permute-start.3 = (bf16[4,96,6,512]{3,0,2,1:T(4,128)(2,1)}, bf16[4,96,6,512]{3,0,2,1:T(4,128)(2,1)}, u32[]{:S(2)}, u32[]{:S(2)}) collective-permute-start(bf16[4,96,6,512]{3,0,2,1:T(4,128)(2,1)} %fusion.30), channel_id=1, source_target_pairs={{0,1},{1,2},{2,3},{3,4},{4,5},{5,6},{6,7},{7,8},{8,9},{9,10},{10,1... | collective-permute-start | bytes 7077896 | tf_op jit(solution)/shard_map/ppermute | solution.py:16
  799.0 58.8 %copy-start.3 = (bf16[512,512]{1,0:T(8,128)(2,1)S(1)}, bf16[512,512]{1,0:T(8,128)(2,1)}, u32[]{:S(2)}) copy-start(bf16[512,512]{1,0:T(8,128)(2,1)} %param.14) | copy-start | bytes 1572868
  857.7 16.5 %copy-start.5 = (f32[512]{0:T(512)S(1)}, f32[512]{0:T(512)}, u32[]{:S(2)}) copy-start(f32[512]{0:T(512)} %param.15) | copy-start | bytes 6148
  874.2 91.8 %copy-start.4 = (bf16[2048,512]{1,0:T(8,128)(2,1)S(1)}, bf16[2048,512]{1,0:T(8,128)(2,1)}, u32[]{:S(2)}) copy-start(bf16[2048,512]{1,0:T(8,128)(2,1)} %param.17) | copy-start | bytes 6291460
  966.0 31.6 %copy-start.1 = (bf16[512,2048]{1,0:T(8,128)(2,1)S(1)}, bf16[512,2048]{1,0:T(8,128)(2,1)}, u32[]{:S(2)}) copy-start(bf16[512,2048]{1,0:T(8,128)(2,1)} %param.16) | copy-start | bytes 6291460
where the time goes:
time: 1000 us; the launch traced here: 998 us
  matrix products  438 us (44%)
  other arithmetic  233 us (23%)
  local copies, waits for them, and re-layouts  222 us (22%)
  waiting for transfers between devices  92.3 us (9%)
  starting transfers between devices  10.9 us (1%)
    reduce_sum x16, other arithmetic, one_band(): jnp.sum(weights, axis=-1, keepdims=True)  204 us
    dot_general x16, matrix products, one_band(): jnp.einsum('aehlrcmsf,amsefhd->alrechd', attn_probs, values_part, preferr...  156 us
    dot_general x16, matrix products, one_band(): jnp.einsum('alrechd,amsefhd->aehlrcmsf', queries, keys_part, preferred_el...  149 us
    ppermute x4, waiting for transfers between devices, from_behind(): lax.ppermute(shard, axis, [(i, (i + by) % count) for i in range(count)])  92.3 us
    dot_general x1, matrix products, per_device(): hidden = jnp.dot(feed_normed, up_weight, preferred_element_type=jnp.float32)  91.7 us
    reshape x16, local copies, waits for them, and re-layouts, one_band(): band.reshape(level_wins, WL, WLAT, col_wins, WLON, 3, heads, head_dim)  29.8 us
    slice x16, local copies, waits for them, and re-layouts, one_band(): values_part = band[:, :, :, :, :, 2]  27.6 us
    dynamic_slice x16, local copies, waits for them, and re-layouts, one_band(): band = lax.dynamic_slice_in_dim(projected, band_start, WLAT, 1)  23.7 us
  transfers between devices with their start and end apart: 4, of which 3 were waited for; matrix products, arithmetic and copies ran while one was open for 3% of the time, Pallas kernels for 0%

commit v1 on v0

v1 whole, which is shorter than its diff:
```python
import functools

import jax
import jax.numpy as jnp
import numpy as np
from jax import lax
from jax.experimental import pallas as pl
from jax.experimental.pallas import tpu as pltpu
from jax.sharding import PartitionSpec as P

WL = 2
WLAT = 6
WLON = 12
HALF_LAT = WLAT // 2
HALF_LON = WLON // 2
EPS = 1e-05
SLABS = 4
HALO = 16
LOG2E = 1.4426950408889634
VMEM_LIMIT = 56 * 1024 * 1024

GELU_POLY = (
    0.7978843450546265,
    0.036333974450826645,
    -3.2892232411541045e-05,
    -5.53166501049418e-05,
    3.98052634409396e-06,
    -1.342210396160226e-07,
    1.8247197086651568e-09,
)


def from_behind(shard, axis, by):
    count = lax.axis_size(axis)
    return lax.ppermute(shard, axis, [(i, (i + by) % count) for i in range(count)])


def norm_rows(values, gain):
    average = jnp.mean(values, axis=-1, keepdims=True)
    centred = values - average
    spread = jnp.mean(centred * centred, axis=-1, keepdims=True)
    return centred * lax.rsqrt(spread + EPS) * gain


def gelu(x):
    u = x * x
    p = jnp.full_like(x, GELU_POLY[-1])
    for c in GELU_POLY[-2::-1]:
        p = p * u + c
    half = 0.5 * x
    return half + half * jnp.tanh(x * p)


def gather_tables(rows):
    wins = rows // WLAT + 1
    piece = SLABS * WLAT
    half = wins // 2
    halfrows = rows // 2

    def pick(w0, w1, r0, r1, halo):
        span = r1 - r0
        table = np.zeros(((w1 - w0) * piece, SLABS * span + (SLABS * HALO if halo else 0)), np.float32)
        for w in range(w0, w1):
            for s in range(SLABS):
                for i in range(WLAT):
                    r = w * WLAT - HALF_LAT + i
                    t = (w - w0) * piece + s * WLAT + i
                    if r < 0:
                        table[t, SLABS * span + s * HALO + r + HALF_LAT] = 1
                    elif r >= rows:
                        table[t, SLABS * span + s * HALO + HALF_LAT + r - rows] = 1
                    else:
                        table[t, s * span + r - r0] = 1
        return table

    first = pick(0, half, 0, halfrows, True)
    middle = pick(half, wins - 1, halfrows - 16, rows, False)
    last = pick(wins - 1, wins, rows - 16, rows, True)

    def place(w0, w1, r0, r1):
        table = np.zeros((SLABS * (r1 - r0), (w1 - w0) * piece), np.float32)
        for s in range(SLABS):
            for r in range(r0, r1):
                w, i = divmod(r + HALF_LAT, WLAT)
                table[s * (r1 - r0) + r - r0, (w - w0) * piece + s * WLAT + i] = 1
        return table

    upper = place(0, half + 1, 0, halfrows)
    lower = place(half, wins, halfrows, rows)
    return [jnp.asarray(t, jnp.bfloat16) for t in (first, middle, last, upper, lower)]


def seam_table():
    i = np.arange(WL * WLON * WLAT) % WLAT < HALF_LAT
    return jnp.asarray(np.where(i[:, None] == i[None, :], 0.0, -1e30), jnp.float32)


def attention_kernel(
    seam_ref, factor_ref, own_ref, recv_ref, halo_own_ref, halo_recv_ref,
    first_ref, middle_ref, last_ref, upper_ref, lower_ref, bias_ref,
    gain_ref, weight_ref, att_own_ref, att_send_ref, xw_ref, aw_ref,
):
    rows, channels = own_ref.shape[2], own_ref.shape[3]
    wins = rows // WLAT + 1
    half = wins // 2
    halfrows = rows // 2
    piece = SLABS * WLAT
    tokens = WL * WLON * WLAT
    heads = factor_ref.shape[0]
    head_dim = channels // heads
    group_heads = 256 // head_dim
    groups = heads // group_heads
    slabs_half = WL * HALF_LON

    def slab(ref, s):
        return ref.at[s // HALF_LON, s % HALF_LON]

    for g in range(2 * slabs_half // SLABS):
        src, halo = (own_ref, halo_own_ref) if g * SLABS < slabs_half else (recv_ref, halo_recv_ref)
        base = g * SLABS % slabs_half
        ids = range(base, base + SLABS)
        edge = [slab(halo, s)[...] for s in ids]
        for table, r0, r1, w0, w1, use_edge in (
            (first_ref, 0, halfrows, 0, half, True),
            (middle_ref, halfrows - 16, rows, half, wins - 1, False),
            (last_ref, rows - 16, rows, wins - 1, wins, True),
        ):
            body = [slab(src, s)[r0:r1, :] for s in ids]
            stacked = jnp.concatenate(body + (edge if use_edge else []), axis=0)
            picked = jnp.dot(table[...], stacked, preferred_element_type=jnp.float32)
            for w in range(w0, w1):
                xw_ref[w, g * piece:(g + 1) * piece, :] = picked[(w - w0) * piece:(w - w0 + 1) * piece]

    lane = lax.broadcasted_iota(jnp.int32, (1, 256), 1) // head_dim
    gain = gain_ref[...]

    def window(w, bias):
        normed = norm_rows(xw_ref[w], gain).astype(jnp.bfloat16)
        projected = jnp.dot(normed, weight_ref[...], preferred_element_type=jnp.float32).astype(jnp.bfloat16)
        for g in range(groups):
            q = projected[:, g * 256:(g + 1) * 256]
            k = projected[:, channels + g * 256:channels + (g + 1) * 256]
            v = projected[:, 2 * channels + g * 256:2 * channels + (g + 1) * 256]
            mixed = jnp.zeros((tokens, 256), jnp.float32)
            for h in range(group_heads):
                mine = lane == h
                qh = q * mine.astype(jnp.bfloat16)
                scores = lax.dot_general(qh, k, (((1,), (1,)), ((), ())), preferred_element_type=jnp.float32)
                if bias is not None:
                    scores = scores + bias
                top = jnp.max(scores, axis=-1, keepdims=True)
                weights = jnp.exp2((scores - top) * factor_ref[g * group_heads + h])
                probs = (weights * (1.0 / jnp.sum(weights, axis=-1, keepdims=True))).astype(jnp.bfloat16)
                out = jnp.dot(probs, v, preferred_element_type=jnp.float32)
                mixed = jnp.where(mine, out, mixed)
            for j in range(2 * slabs_half // SLABS):
                aw_ref[j, pl.ds(pl.multiple_of(w * piece, 8), piece), g * 256:(g + 1) * 256] = mixed[j * piece:(j + 1) * piece]

    def inner(w, carry):
        window(w, None)
        return carry

    window(0, bias_ref[...] * seam_ref[0])
    lax.fori_loop(1, wins - 1, inner, 0)
    window(wins - 1, bias_ref[...] * seam_ref[1])

    for g in range(2 * slabs_half // SLABS):
        dst = att_own_ref if g * SLABS < slabs_half else att_send_ref
        base = g * SLABS % slabs_half
        for table, r0, w0, w1 in ((upper_ref, 0, 0, half + 1), (lower_ref, halfrows, half, wins)):
            source = aw_ref[g, w0 * piece:w1 * piece, :].astype(jnp.bfloat16)
            placed = jnp.dot(table[...], source, preferred_element_type=jnp.float32).astype(jnp.bfloat16)
            for n, s in enumerate(range(base, base + SLABS)):
                slab(dst, s)[r0:r0 + halfrows, :] = placed[n * halfrows:(n + 1) * halfrows]


def attention(pair, seam, factor, latent, recv, halo, halo_recv, tables, bias, gain, weight):
    levels, cols, rows, channels = latent.shape
    wins = rows // WLAT + 1
    full = lambda a: pl.BlockSpec(a.shape, lambda i, n=a.ndim: (0,) * n)
    smem = pl.BlockSpec(memory_space=pltpu.SMEM)
    own = lambda r: pl.BlockSpec((WL, HALF_LON, r, channels), lambda i: (pair, 1, 0, 0))
    other = lambda r: pl.BlockSpec((WL, HALF_LON, r, channels), lambda i: (0, 0, 0, 0))
    out = jax.ShapeDtypeStruct((WL, HALF_LON, rows, channels), jnp.bfloat16)
    return pl.pallas_call(
        attention_kernel,
        grid=(1,),
        out_shape=(out, out),
        in_specs=[smem, smem, own(rows), other(rows), own(HALO), other(HALO)]
        + [full(t) for t in tables] + [full(bias), full(gain), full(weight)],
        out_specs=(other(rows), other(rows)),
        scratch_shapes=[
            pltpu.VMEM((wins, WL * WLON * WLAT, channels), jnp.float32),
            pltpu.VMEM((WL * WLON // SLABS, wins * SLABS * WLAT, channels), jnp.float32),
        ],
        compiler_params=pltpu.CompilerParams(vmem_limit_bytes=VMEM_LIMIT),
        cost_estimate=pl.CostEstimate(flops=8_000_000_000, bytes_accessed=8_000_000, transcendentals=5_000_000),
    )(seam, factor, latent, recv, halo, halo_recv, *tables, bias, gain, weight)


def feed_kernel(att_ref, latent_ref, wo_ref, gain_ref, up_ref, down_ref, *rest):
    out_ref = rest[-1]
    channels = latent_ref.shape[-1]
    hidden = up_ref.shape[1]
    block = 512
    shape = latent_ref.shape
    att = att_ref[...].reshape(-1, channels)
    residual = latent_ref[...].reshape(-1, channels).astype(jnp.float32) + jnp.dot(
        att, wo_ref[...], preferred_element_type=jnp.float32
    )
    normed = norm_rows(residual, gain_ref[...]).astype(jnp.bfloat16)
    total = residual
    for b in range(0, hidden, block):
        act = gelu(jnp.dot(normed, up_ref[:, b:b + block], preferred_element_type=jnp.float32))
        total = total + jnp.dot(act.astype(jnp.bfloat16), down_ref[b:b + block, :], preferred_element_type=jnp.float32)
    out_ref[...] = total.astype(jnp.bfloat16).reshape(shape)


def feed(pair, side, att, latent, wo, gain, up, down, out):
    levels, cols, rows, channels = latent.shape
    step = 3
    steps = HALF_LON // step
    full = lambda a: pl.BlockSpec(a.shape, lambda i, j, n=a.ndim: (0,) * n)
    place = pl.BlockSpec((1, step, rows, channels), lambda i, j: (WL * pair + i, steps * side + j, 0, 0))
    local = pl.BlockSpec((1, step, rows, channels), lambda i, j: (i, j, 0, 0))
    operands = [att, latent, wo, gain, up, down]
    specs = [local, place, full(wo), full(gain), full(up), full(down)]
    aliases = {}
    if out is not None:
        operands.append(out)
        specs.append(pl.BlockSpec(memory_space=pl.ANY))
        aliases = {len(operands) - 1: 0}
    return pl.pallas_call(
        feed_kernel,
        grid=(WL, steps),
        out_shape=jax.ShapeDtypeStruct(latent.shape, jnp.bfloat16),
        in_specs=specs,
        out_specs=place,
        input_output_aliases=aliases,
        compiler_params=pltpu.CompilerParams(vmem_limit_bytes=VMEM_LIMIT),
        cost_estimate=pl.CostEstimate(flops=6_000_000_000, bytes_accessed=8_000_000, transcendentals=2_400_000),
    )(*operands)


def per_device(
    latent,
    attention_gain,
    triple_weight,
    head_scale,
    output_weight,
    feed_gain,
    up_weight,
    down_weight,
):
    x = latent.transpose(0, 2, 1, 3)
    levels, cols, rows, channels = x.shape
    head_dim = channels // head_scale.shape[0]
    pairs = levels // WL
    lat = lax.axis_index("lat")
    count = lax.axis_size("lat")
    seam = jnp.stack([lat == 0, lat == count - 1]).astype(jnp.float32)
    factor = head_scale * (LOG2E / head_dim ** 0.5)
    tables = gather_tables(rows)
    bias = seam_table()
    gain = attention_gain.reshape(1, -1)
    gain2 = feed_gain.reshape(1, -1)

    above = from_behind(x[:, :, rows - HALF_LAT:], "lat", 1)
    below = from_behind(x[:, :, :HALF_LAT], "lat", -1)
    edges = jnp.concatenate([above, below], axis=2)
    edges_recv = from_behind(edges[:, :HALF_LON], "lon", -1)
    pad = ((0, 0), (0, 0), (0, HALO - 2 * HALF_LAT), (0, 0))
    halo = jnp.pad(edges, pad)
    halo_recv = jnp.pad(edges_recv, pad)
    recv = [from_behind(x[WL * p:WL * p + WL, :HALF_LON], "lon", -1) for p in range(pairs)]
    out = None
    returned = []
    for p in range(pairs):
        own, send = attention(
            p, seam, factor, x, recv[p], halo, halo_recv[WL * p:WL * p + WL], tables, bias, gain, triple_weight
        )
        returned.append(from_behind(send, "lon", 1))
        out = feed(p, 1, own, x, output_weight, gain2, up_weight, down_weight, out)
    for p in range(pairs):
        out = feed(p, 0, returned[p], x, output_weight, gain2, up_weight, down_weight, out)
    return out.transpose(0, 2, 1, 3)


def solution(mesh):
    in_specs = (P(None, "lat", "lon", None), P(), P(), P(), P(), P(), P(), P())
    out_specs = P(None, "lat", "lon", None)
    return jax.shard_map(
        per_device, mesh=mesh, in_specs=in_specs, out_specs=out_specs, check_vma=False
    )
```

time: 1000 us -> 203 us (0.20)
  matrix products: 438 us -> 0 us
  other arithmetic: 233 us -> 1.41 us
  local copies, waits for them, and re-layouts: 222 us -> 7 us
  Pallas kernels: 0 us -> 123 us
  waiting for transfers between devices: 92.3 us -> 6.7 us
  starting transfers between devices: 10.9 us -> 62.4 us
    dot_general x36 -> x0, matrix products: 438 us -> none  [the longest x16 156 us: one_band(): jnp.einsum('aehlrcmsf,amsefhd->alrechd', attn_probs, values_part, preferr...]
    reduce_sum x19 -> x0, other arithmetic: 214 us -> none  [the longest x16 204 us: one_band(): jnp.sum(weights, axis=-1, keepdims=True)]
    pallas_call x0 -> x6, Pallas kernels: none -> 123 us  [the longest x4 65.6 us: feed(): pl.pallas_call(feed_kernel, grid=(WL, steps), out_shape=jax.ShapeDtypeStr...]
    reshape x37 -> x0, local copies, waits for them, and re-layouts: 89.3 us -> none  [the longest x16 29.8 us: one_band(): band.reshape(level_wins, WL, WLAT, col_wins, WLON, 3, heads, head_dim)]
    ppermute x4 -> x7, waiting for transfers between devices: 92.3 us -> 6.7 us  [from_behind(): lax.ppermute(shard, axis, [(i, (i + by) % count) for i in range(count)])]
    ppermute x4 -> x7, starting transfers between devices: 10.9 us -> 62.4 us  [from_behind(): lax.ppermute(shard, axis, [(i, (i + by) % count) for i in range(count)])]
    slice x19 -> x3, local copies, waits for them, and re-layouts: 36.1 us -> 3.91 us  [the longest x1 1.84 us: per_device(): x[WL * p:WL * p + WL, :HALF_LON]]
    convert_element_type x18 -> x0, local copies, waits for them, and re-layouts: 25.4 us -> none  [the longest x2 19.3 us: per_device(): inputs.astype(jnp.float32)]
  transfers between devices with their start and end apart: 4 -> 7, of which waited for: 3 -> 3; matrix products, arithmetic and copies ran while one was open for 3% -> 2% of each run, Pallas kernels for 0% -> 53%
where the time goes in v1:
time: 203 us; the launch traced here: 200 us
  Pallas kernels  123 us (61%)
  starting transfers between devices  62.4 us (31%)
  local copies, waits for them, and re-layouts  7 us (3%)
  waiting for transfers between devices  6.7 us (3%)
    pallas_call x4, Pallas kernels, feed(): pl.pallas_call(feed_kernel, grid=(WL, steps), out_shape=jax.ShapeDtypeStr...  65.6 us
    ppermute x7, starting transfers between devices, from_behind(): lax.ppermute(shard, axis, [(i, (i + by) % count) for i in range(count)])  62.4 us
    pallas_call x2, Pallas kernels, attention(): pl.pallas_call(attention_kernel, grid=(1,), out_shape=(out, out), in_spec...  57.2 us
    ppermute x7, waiting for transfers between devices, from_behind(): lax.ppermute(shard, axis, [(i, (i + by) % count) for i in range(count)])  6.7 us
  transfers between devices with their start and end apart: 7, of which 3 were waited for; matrix products, arithmetic and copies ran while one was open for 2% of the time, Pallas kernels for 53%

profile of v1, /device:TPU:1, one launch (start us, length us, event | category | flops | bytes accessed | tf_op | source)
XLA Modules:
  0.0 200.3 jit_solution(8745664208425304800)
XLA Ops:
  0.0 0.0 copy-start.2
  0.0 1.8 fusion.1
  1.8 9.1 %collective-permute-start.5 = (bf16[2,6,96,512]{3,2,1,0:T(8,128)(2,1)S(1)}, bf16[2,6,96,512]{3,2,1,0:T(8,128)(2,1)}, u32[]{:S(2)}, u32[]{:S(2)}) collective-permute-start(bf16[2,6,96,512]{3,2,1,0:T(8,128)(2,1)S(1)} %get-tuple-element.13), channel_id=1, source_target_pairs={{0,31},{1,0},{2,1},{3,2},{4,3},{5,4},{6,5},{7,6},{8,7},{9,8},{10,9... | collective-permute-start | bytes 3538952 | tf_op jit(solution)/shard_map/ppermute | solution.py:35
  11.0 1.3 fusion.2
  12.3 1.6 collective-permute-start.1
  13.9 0.0 collective-permute-start.2
  13.9 1.2 collective-permute-start
  15.1 0.0 copy-done.2
  15.1 0.5 broadcast_multiply_fusion.factor_ref
  15.6 1.7 collective-permute-done.1
  17.3 2.9 %collective-permute-done.2 = bf16[4,12,3,512]{3,2,1,0:T(4,128)(2,1)S(1)} collective-permute-done((bf16[4,12,3,512]{3,2,1,0:T(4,128)(2,1)S(1)}, bf16[4,12,3,512]{3,2,1,0:T(4,128)(2,1)S(1)}, u32[]{:S(2)}, u32[]{:S(2)}) %collective-permute-start.2) | collective-permute-done | bytes 147488 | tf_op jit(solution)/shard_map/ppermute | solution.py:35
  20.2 0.1 fusion
  20.3 50.5 %collective-permute-start.3 = (bf16[4,6,6,512]{3,2,1,0:T(8,128)(2,1)S(1)}, bf16[4,6,6,512]{3,2,1,0:T(8,128)(2,1)S(1)}, u32[]{:S(2)}, u32[]{:S(2)}) collective-permute-start(bf16[4,6,6,512]{3,2,1,0:T(8,128)(2,1)S(1)} %fusion), channel_id=1, source_target_pairs={{0,31},{1,0},{2,1},{3,2},{4,3},{5,4},{6,5},{7,6},{8,7},{9,8},{10,9... | collective-permute-start | bytes 442376 | tf_op jit(solution)/shard_map/ppermute | solution.py:35
  70.8 0.6 add_convert_fusion.seam_ref
  71.4 0.2 pad_maximum_fusion
  71.6 1.0 pad.8.halo_own_ref
  72.6 2.1 %collective-permute-done.3 = bf16[4,6,6,512]{3,2,1,0:T(8,128)(2,1)S(1)} collective-permute-done((bf16[4,6,6,512]{3,2,1,0:T(8,128)(2,1)S(1)}, bf16[4,6,6,512]{3,2,1,0:T(8,128)(2,1)S(1)}, u32[]{:S(2)}, u32[]{:S(2)}) %collective-permute-start.3) | collective-permute-done | bytes 147488 | tf_op jit(solution)/shard_map/ppermute | solution.py:35
  74.7 0.8 pad_slice_fusion.2
  75.5 0.0 collective-permute-done.5.recv_ref
  75.5 28.6 %shard_map.137 = (bf16[2,6,96,512]{3,2,1,0:T(8,128)(2,1)}, bf16[2,6,96,512]{3,2,1,0:T(8,128)(2,1)}) custom-call(f32[2]{0:T(128)} %add_convert_fusion.seam_ref, f32[8]{0:T(128)} %broadcast_multiply_fusion.factor_ref, bf16[4,12,96,512]{3,2,1,0:T(8,128)(2,1)} %bitcast.8, bf16[2,6,96,512]{3,2,1,0:T(8,128)(2,1)} %collective-permute-done.5.recv_ref, ...), custom_call_target="tpu_custom_call" | custom-call | flops 8000000000 | bytes 8000000 | tf_op jit(solution)/shard_map/pallas_call | solution.py:185
  104.1 0.0 collective-permute-start.6
  104.1 0.0 collective-permute-done.recv_ref
  104.1 28.6 %shard_map.136 = (bf16[2,6,96,512]{3,2,1,0:T(8,128)(2,1)}, bf16[2,6,96,512]{3,2,1,0:T(8,128)(2,1)}) custom-call(f32[2]{0:T(128)} %add_convert_fusion.seam_ref, f32[8]{0:T(128)} %broadcast_multiply_fusion.factor_ref, bf16[4,12,96,512]{3,2,1,0:T(8,128)(2,1)} %bitcast.9, bf16[2,6,96,512]{3,2,1,0:T(8,128)(2,1)} %collective-permute-done.recv_ref, ...), custom_call_target="tpu_custom_call" | custom-call | flops 8000000000 | bytes 8000000 | tf_op jit(solution)/shard_map/pallas_call | solution.py:185
  132.7 0.0 collective-permute-start.4
  132.7 16.4 %shard_map.138.rest_0_ = bf16[4,12,96,512]{3,2,1,0:T(8,128)(2,1)} custom-call(bf16[2,6,96,512]{3,2,1,0:T(8,128)(2,1)} %get-tuple-element.12.att_ref, bf16[4,12,96,512]{3,2,1,0:T(8,128)(2,1)} %bitcast.10, bf16[512,512]{1,0:T(8,128)(2,1)} %wo_ref.7, f32[1,512]{1,0:T(1,128)} %bitcast.16, bf16[512,2048]{1,0:T(8,128)(2,1)} %up_ref.7, bf16[2048,512]{1,0:T(8,128)(2,1)} %down_ref.7), custom_call_target="tpu_custom_call" | custom-call | flops 6000000000 | bytes 8000000 | tf_op jit(solution)/shard_map/pallas_call | solution.py:233
  149.1 16.4 %shard_map.139.rest_0_ = bf16[4,12,96,512]{3,2,1,0:T(8,128)(2,1)} custom-call(bf16[2,6,96,512]{3,2,1,0:T(8,128)(2,1)} %get-tuple-element.11.att_ref, bf16[4,12,96,512]{3,2,1,0:T(8,128)(2,1)} %bitcast.11, bf16[512,512]{1,0:T(8,128)(2,1)} %wo_ref.7, f32[1,512]{1,0:T(1,128)} %bitcast.17, bf16[512,2048]{1,0:T(8,128)(2,1)} %up_ref.7, ...), custom_call_target="tpu_custom_call", output_to_operand_aliasing={{}: (6, {})} | custom-call | flops 6000000000 | bytes 8000000 | tf_op jit(solution)/shard_map/pallas_call | solution.py:233
  165.5 0.0 collective-permute-done.6.att_ref
  165.5 0.0 copy-start
  165.5 1.0 copy-done
  166.5 16.4 %shard_map.140.rest_0_ = bf16[4,12,96,512]{3,2,1,0:T(8,128)(2,1)} custom-call(bf16[2,6,96,512]{3,2,1,0:T(8,128)(2,1)} %copy-done, bf16[4,12,96,512]{3,2,1,0:T(8,128)(2,1)} %bitcast.12, bf16[512,512]{1,0:T(8,128)(2,1)} %wo_ref.7, f32[1,512]{1,0:T(1,128)} %bitcast.18, bf16[512,2048]{1,0:T(8,128)(2,1)} %up_ref.7, ...), custom_call_target="tpu_custom_call", output_to_operand_aliasing={{}: (6, {})} | custom-call | flops 6000000000 | bytes 8000000 | tf_op jit(solution)/shard_map/pallas_call | solution.py:233
  182.9 0.0 collective-permute-done.4.att_ref
  182.9 0.0 copy-start.1
  182.9 1.0 copy-done.1
  183.9 16.4 %shard_map.141 = bf16[4,12,96,512]{3,2,1,0:T(8,128)(2,1)} custom-call(bf16[2,6,96,512]{3,2,1,0:T(8,128)(2,1)} %copy-done.1, bf16[4,12,96,512]{3,2,1,0:T(8,128)(2,1)} %bitcast.13, bf16[512,512]{1,0:T(8,128)(2,1)} %wo_ref.7, f32[1,512]{1,0:T(1,128)} %bitcast.19, bf16[512,2048]{1,0:T(8,128)(2,1)} %up_ref.7, ...), custom_call_target="tpu_custom_call", output_to_operand_aliasing={{}: (6, {})} | custom-call | flops 6000000000 | bytes 8000000 | tf_op jit(solution)/shard_map/pallas_call | solution.py:233
Async XLA Ops:
  0.0 15.1 %copy-start.2 = (f32[8]{0:T(128)S(1)}, f32[8]{0:T(128)}, u32[]{:S(2)}) copy-start(f32[8]{0:T(128)} %param.17) | copy-start | bytes 100
  1.8 73.6 %collective-permute-start.5 = (bf16[2,6,96,512]{3,2,1,0:T(8,128)(2,1)S(1)}, bf16[2,6,96,512]{3,2,1,0:T(8,128)(2,1)}, u32[]{:S(2)}, u32[]{:S(2)}) collective-permute-start(bf16[2,6,96,512]{3,2,1,0:T(8,128)(2,1)S(1)} %get-tuple-element.13), channel_id=1, source_target_pairs={{0,31},{1,0},{2,1},{3,2},{4,3},{5,4},{6,5},{7,6},{8,7},{9,8},{10,9... | collective-permute-start | bytes 3538952 | tf_op jit(solution)/shard_map/ppermute | solution.py:35
  12.3 5.0 %collective-permute-start.1 = (bf16[4,12,3,512]{3,2,1,0:T(4,128)(2,1)S(1)}, bf16[4,12,3,512]{3,2,1,0:T(4,128)(2,1)S(1)}, u32[]{:S(2)}, u32[]{:S(2)}) collective-permute-start(bf16[4,12,3,512]{3,2,1,0:T(4,128)(2,1)S(1)} %get-tuple-element.15), channel_id=1, source_target_pairs={{0,32},{32,64},{64,96},{96,0},{1,33},{33,65},{65,97},{97,1},{2,34}... | collective-permute-start | bytes 442376 | tf_op jit(solution)/shard_map/ppermute | solution.py:35
  13.9 6.3 %collective-permute-start.2 = (bf16[4,12,3,512]{3,2,1,0:T(4,128)(2,1)S(1)}, bf16[4,12,3,512]{3,2,1,0:T(4,128)(2,1)S(1)}, u32[]{:S(2)}, u32[]{:S(2)}) collective-permute-start(bf16[4,12,3,512]{3,2,1,0:T(4,128)(2,1)S(1)} %get-tuple-element.16), channel_id=1, source_target_pairs={{0,96},{32,0},{64,32},{96,64},{1,97},{33,1},{65,33},{97,65},{2,98}... | collective-permute-start | bytes 442376 | tf_op jit(solution)/shard_map/ppermute | solution.py:35
  13.9 90.2 %collective-permute-start = (bf16[2,6,96,512]{3,2,1,0:T(8,128)(2,1)S(1)}, bf16[2,6,96,512]{3,2,1,0:T(8,128)(2,1)}, u32[]{:S(2)}, u32[]{:S(2)}) collective-permute-start(bf16[2,6,96,512]{3,2,1,0:T(8,128)(2,1)S(1)} %get-tuple-element.14), channel_id=1, source_target_pairs={{0,31},{1,0},{2,1},{3,2},{4,3},{5,4},{6,5},{7,6},{8,7},{9,8},{10,9... | collective-permute-start | bytes 3538952 | tf_op jit(solution)/shard_map/ppermute | solution.py:35
  20.3 54.4 %collective-permute-start.3 = (bf16[4,6,6,512]{3,2,1,0:T(8,128)(2,1)S(1)}, bf16[4,6,6,512]{3,2,1,0:T(8,128)(2,1)S(1)}, u32[]{:S(2)}, u32[]{:S(2)}) collective-permute-start(bf16[4,6,6,512]{3,2,1,0:T(8,128)(2,1)S(1)} %fusion), channel_id=1, source_target_pairs={{0,31},{1,0},{2,1},{3,2},{4,3},{5,4},{6,5},{7,6},{8,7},{9,8},{10,9... | collective-permute-start | bytes 442376 | tf_op jit(solution)/shard_map/ppermute | solution.py:35
  104.1 61.4 %collective-permute-start.6 = (bf16[2,6,96,512]{3,2,1,0:T(8,128)(2,1)}, bf16[2,6,96,512]{3,2,1,0:T(8,128)(2,1)S(1)}, u32[]{:S(2)}, u32[]{:S(2)}) collective-permute-start(bf16[2,6,96,512]{3,2,1,0:T(8,128)(2,1)} %get-tuple-element.10), channel_id=1, source_target_pairs={{0,1},{1,2},{2,3},{3,4},{4,5},{5,6},{6,7},{7,8},{8,9},{9,10},{10,1... | collective-permute-start | bytes 3538952 | tf_op jit(solution)/shard_map/ppermute | solution.py:35
  132.7 50.2 %collective-permute-start.4 = (bf16[2,6,96,512]{3,2,1,0:T(8,128)(2,1)}, bf16[2,6,96,512]{3,2,1,0:T(8,128)(2,1)S(1)}, u32[]{:S(2)}, u32[]{:S(2)}) collective-permute-start(bf16[2,6,96,512]{3,2,1,0:T(8,128)(2,1)} %get-tuple-element.9), channel_id=1, source_target_pairs={{0,1},{1,2},{2,3},{3,4},{4,5},{5,6},{6,7},{7,8},{8,9},{9,10},{10,1... | collective-permute-start | bytes 3538952 | tf_op jit(solution)/shard_map/ppermute | solution.py:35
  165.5 1.0 copy-start
  182.9 1.0 copy-start.1

commit v2 on v0

v2 whole, which is shorter than its diff:
```python
import functools

import jax
import jax.numpy as jnp
import numpy as np
from jax import lax
from jax.experimental import pallas as pl
from jax.experimental.pallas import tpu as pltpu
from jax.sharding import PartitionSpec as P

WL = 2
WLAT = 6
WLON = 12
HALF_LAT = WLAT // 2
HALF_LON = WLON // 2
EPS = 1e-05
SLABS = 4
PIECE = SLABS * WLAT
SIDE_SLABS = WL * HALF_LON
SIDE = SIDE_SLABS * WLAT
TOKENS = 2 * SIDE
GROUPS = SIDE_SLABS // SLABS
TILE = 16
THIRD = 32
LOG2E = 1.4426950408889634
VMEM_LIMIT = 36 * 1024 * 1024


def from_behind(shard, axis, by):
    count = lax.axis_size(axis)
    return lax.ppermute(shard, axis, [(i, (i + by) % count) for i in range(count)])


def norm_rows(values, gain):
    average = jnp.mean(values, axis=-1, keepdims=True)
    centred = values - average
    spread = jnp.mean(centred * centred, axis=-1, keepdims=True)
    return centred * lax.rsqrt(spread + EPS) * gain


def gelu(x):
    half = 0.5 * x
    return half + half * lax.erf(x * 0.7071067811865476)


class Part:
    def __init__(self, half, rows):
        self.half = half
        self.rows = rows
        self.mid = rows // 2
        total = rows // WLAT + 1
        cut = total // 2
        self.bands = list(range(cut)) if half == 0 else list(range(cut, total))
        self.first_kept = THIRD // WLAT
        self.carried = cut - self.first_kept
        low, main, edge = ("low", self.mid - TILE, self.mid), ("main", half * self.mid, (half + 1) * self.mid), ("edge", 0, 0)
        if half == 0:
            self.picks = [(self.bands, [main, edge])]
            self.places = [(0, THIRD, 0, cut)]
            self.offset = 0
        else:
            self.picks = [(self.bands[:-1], [low, main]), (self.bands[-1:], [("main", rows - TILE, rows), edge])]
            self.places = [(r, r + THIRD, self.first_kept, total) for r in range(THIRD, rows, THIRD)]
            self.offset = self.carried
        self.stored = len(self.bands) + self.offset
        self.tables = [self.pick_table(b, s) for b, s in self.picks] + [self.place_table(*p)[0] for p in self.places]

    def pick_table(self, bands, segments):
        width = sum(SLABS * (r1 - r0 if name != "edge" else TILE) for name, r0, r1 in segments)
        table = np.zeros((len(bands) * PIECE, width), np.float32)
        for n, band in enumerate(bands):
            for s in range(SLABS):
                for i in range(WLAT):
                    r = band * WLAT - HALF_LAT + i
                    start = 0
                    for name, r0, r1 in segments:
                        span = TILE if name == "edge" else r1 - r0
                        if name != "edge" and r0 <= r < r1:
                            table[n * PIECE + s * WLAT + i, start + s * span + r - r0] = 1
                        elif name == "edge" and r < 0:
                            table[n * PIECE + s * WLAT + i, start + s * span + r + HALF_LAT] = 1
                        elif name == "edge" and r >= self.rows:
                            table[n * PIECE + s * WLAT + i, start + s * span + r - self.rows + HALF_LAT] = 1
                        start += SLABS * span
        return jnp.asarray(table, jnp.bfloat16)

    def place_table(self, r0, r1, base, end):
        b0, b1 = (r0 + HALF_LAT) // WLAT, (r1 - 1 + HALF_LAT) // WLAT + 1
        table = np.zeros((SLABS * (r1 - r0), (b1 - b0) * PIECE), np.float32)
        for s in range(SLABS):
            for r in range(r0, r1):
                band, i = divmod(r + HALF_LAT, WLAT)
                table[s * (r1 - r0) + r - r0, (band - b0) * PIECE + s * WLAT + i] = 1
        return jnp.asarray(table, jnp.bfloat16), b0 - base, b1 - base


def seam_table():
    i = np.arange(TOKENS) % WLAT < HALF_LAT
    return jnp.asarray(np.where(i[:, None] == i[None, :], 0.0, -1e30), jnp.float32)


def block_kernel(part, pair, aliased, *refs):
    refs = list(refs)
    pop = lambda: refs.pop(0)
    seam_ref, factor_ref = pop(), pop()
    source = {name: (pop(), pop(), pop()) for name in (("main", "edge") if part.half == 0 else ("main", "edge", "low"))}
    pick_refs = [pop() for _ in part.picks]
    place_refs = [pop() for _ in part.places]
    bias_ref, gain_ref, gain2_ref = pop(), pop(), pop()
    carry_in = pop() if part.half == 1 else None
    weights_hbm = [pop() for _ in range(4)]
    if aliased:
        pop()
    out_ref = pop()
    carry_out = pop() if part.half == 0 else None
    weights = [pop() for _ in range(4)]
    xw_ref, hw_ref, att_ref, yw_ref, ow_ref, wsem, osem = refs
    qkv_ref, wo_ref, up_ref, down_ref = weights
    channels = xw_ref.shape[-1]
    heads = factor_ref.shape[0]
    head_dim = channels // heads
    group_heads = 256 // head_dim
    count = len(part.bands)
    main0 = part.half * part.mid

    copies = [pltpu.make_async_copy(a, b, wsem.at[i]) for i, (a, b) in enumerate(zip(weights_hbm, weights))]
    for copy in copies:
        copy.start()

    for dest, side in ((xw_ref, 0), (xw_ref, 1), (hw_ref, 0), (hw_ref, 1)):
        own = dest is xw_ref

        def rows_of(name, s, r0, r1):
            ref = source[name][0 if own else 1 + side]
            col = s % HALF_LON + (side * HALF_LON if own else 0)
            base = {"main": main0, "low": part.mid - TILE, "edge": 0}[name]
            if name == "edge":
                r0, r1 = 0, TILE
            return ref[s // HALF_LON, col, r0 - base:r1 - base, :]

        for g in range(GROUPS):
            ids = range(g * SLABS, (g + 1) * SLABS)
            for table, (bands, segments) in zip(pick_refs, part.picks):
                stacked = jnp.concatenate([rows_of(n, s, r0, r1) for n, r0, r1 in segments for s in ids], axis=0)
                picked = jnp.dot(table[...], stacked, preferred_element_type=jnp.float32)
                for n, band in enumerate(bands):
                    at = (side * GROUPS + g) * PIECE
                    dest[band - part.bands[0], at:at + PIECE, :] = picked[n * PIECE:(n + 1) * PIECE]

    lane = lax.broadcasted_iota(jnp.int32, (1, 256), 1) // head_dim
    gain, gain2 = gain_ref[...], gain2_ref[...]
    copies[0].wait()

    def attend(b, bias):
        normed = norm_rows(xw_ref[b], gain).astype(jnp.bfloat16)
        around = norm_rows(hw_ref[b], gain).astype(jnp.bfloat16)
        mine = jnp.dot(normed, qkv_ref[...], preferred_element_type=jnp.float32)
        other = jnp.dot(around, qkv_ref[:, channels:], preferred_element_type=jnp.float32)
        for g in range(heads // group_heads):
            at = g * 256
            mixed = []
            for side in (0, 1):
                rows = slice(side * SIDE, (side + 1) * SIDE)
                q = mine[rows, at:at + 256]
                k, v = [
                    jnp.concatenate(
                        [mine[rows, c * channels + at:c * channels + at + 256],
                         other[rows, (c - 1) * channels + at:(c - 1) * channels + at + 256]], axis=0
                    ).astype(jnp.bfloat16)
                    for c in (1, 2)
                ]
                stacked = jnp.concatenate([jnp.where(lane == h, q, 0.0) for h in range(group_heads)], axis=0)
                scores = lax.dot_general(
                    stacked.astype(jnp.bfloat16), k, (((1,), (1,)), ((), ())), preferred_element_type=jnp.float32
                )
                probs = []
                for h in range(group_heads):
                    s = scores[h * SIDE:(h + 1) * SIDE]
                    if bias is not None:
                        s = s + bias[:SIDE]
                    top = jnp.max(s, axis=-1, keepdims=True)
                    e = jnp.exp2((s - top) * factor_ref[g * group_heads + h])
                    probs.append(e * (1.0 / jnp.sum(e, axis=-1, keepdims=True)))
                probs = jnp.concatenate(probs, axis=0).astype(jnp.bfloat16)
                out = jnp.dot(probs, v, preferred_element_type=jnp.float32)
                total = out[:SIDE]
                for h in range(1, group_heads):
                    total = jnp.where(lane == h, out[h * SIDE:(h + 1) * SIDE], total)
                mixed.append(total)
            att_ref[b, :, at:at + 256] = jnp.concatenate(mixed, axis=0).astype(jnp.bfloat16)

    def feed(b):
        residual = xw_ref[b] + jnp.dot(att_ref[b], wo_ref[...], preferred_element_type=jnp.float32)
        normed = norm_rows(residual, gain2).astype(jnp.bfloat16)
        acts = gelu(jnp.dot(normed, up_ref[...], preferred_element_type=jnp.float32)).astype(jnp.bfloat16)
        result = residual + jnp.dot(acts, down_ref[...], preferred_element_type=jnp.float32)
        at = (b + part.offset) * PIECE
        at = at if isinstance(b, int) else pl.multiple_of(at, 8)
        for g in range(2 * GROUPS):
            yw_ref[g, pl.ds(at, PIECE), :] = result[g * PIECE:(g + 1) * PIECE]

    bias = bias_ref[...] * seam_ref[part.half]
    if part.half == 0:
        attend(0, bias)
    else:
        attend(0, None)
    for copy in copies[1:]:
        copy.wait()
    if part.half == 1:
        for g in range(2 * GROUPS):
            yw_ref[g, :part.carried * PIECE, :] = carry_in[g]

    def step(b, carry):
        feed(b - 1)
        attend(b, None)
        return carry

    if part.half == 0:
        lax.fori_loop(1, count, step, 0)
    else:
        lax.fori_loop(1, count - 1, step, 0)
        feed(count - 2)
        attend(count - 1, bias)
    feed(count - 1)

    for table, spec in zip(place_refs, part.places):
        r0, r1 = spec[:2]
        b0, b1 = (r0 + HALF_LAT) // WLAT, (r1 - 1 + HALF_LAT) // WLAT + 1
        for g in range(2 * GROUPS):
            band_rows = yw_ref[g, (b0 - spec[2]) * PIECE:(b1 - spec[2]) * PIECE, :].astype(jnp.bfloat16)
            placed = jnp.dot(table[...], band_rows, preferred_element_type=jnp.float32).astype(jnp.bfloat16)
            for n in range(SLABS):
                s = g % GROUPS * SLABS + n
                col = s % HALF_LON + g // GROUPS * HALF_LON
                ow_ref[s // HALF_LON, col, r0 - part.places[0][0]:r1 - part.places[0][0], :] = placed[n * THIRD:(n + 1) * THIRD]
    if carry_out is not None:
        for g in range(2 * GROUPS):
            carry_out[g] = yw_ref[g, part.first_kept * PIECE:(part.first_kept + part.carried) * PIECE, :]
    copy = pltpu.make_async_copy(
        ow_ref,
        out_ref.at[pl.ds(WL * pair, WL), :, pl.ds(part.places[0][0], ow_ref.shape[2]), :],
        osem,
    )
    copy.start()
    copy.wait()


def block(part, pair, seam, factor, x, pieces, edges, bias, gains, carry, weights, out):
    levels, cols, rows, channels = x.shape
    mid, half = part.mid, part.half
    whole = lambda a: pl.BlockSpec(a.shape, lambda i, n=a.ndim: (0,) * n)
    smem = pl.BlockSpec(memory_space=pltpu.SMEM)
    hbm = pl.BlockSpec(memory_space=pl.ANY)
    spec = lambda n, r, p, at: pl.BlockSpec((WL, n, r, channels), lambda i: (p, 0, at, 0))
    operands = [seam, factor]
    specs = [smem, smem]
    operands += [x, *pieces[half]]
    specs += [spec(cols, mid, pair, half), spec(HALF_LON, mid, 0, 0), spec(HALF_LON, mid, 0, 0)]
    operands += edges
    specs += [spec(cols, TILE, pair, 0), spec(HALF_LON, TILE, pair, 0), spec(HALF_LON, TILE, pair, 0)]
    if half == 1:
        at = mid // TILE - 1
        operands += [x, *pieces[0]]
        specs += [spec(cols, TILE, pair, at), spec(HALF_LON, TILE, 0, at), spec(HALF_LON, TILE, 0, at)]
    small = [*part.tables, bias, *gains] + ([carry] if half == 1 else [])
    operands += small
    specs += [whole(a) for a in small]
    operands += weights
    specs += [hbm] * len(weights)
    aliases = {}
    if out is not None:
        aliases = {len(operands): 0}
        operands.append(out)
        specs.append(hbm)
    shape = jax.ShapeDtypeStruct(x.shape, jnp.bfloat16)
    if half == 0:
        kept = jax.ShapeDtypeStruct((2 * GROUPS, part.carried * PIECE, channels), jnp.float32)
        out_shape, out_specs = (shape, kept), (hbm, whole(kept))
    else:
        out_shape, out_specs = shape, hbm
    count = len(part.bands)
    return pl.pallas_call(
        functools.partial(block_kernel, part, pair, out is not None),
        grid=(1,),
        out_shape=out_shape,
        in_specs=specs,
        out_specs=out_specs,
        scratch_shapes=[pltpu.VMEM(w.shape, w.dtype) for w in weights]
        + [
            pltpu.VMEM((count, TOKENS, channels), jnp.float32),
            pltpu.VMEM((count, TOKENS, channels), jnp.float32),
            pltpu.VMEM((count, TOKENS, channels), jnp.bfloat16),
            pltpu.VMEM((2 * GROUPS, part.stored * PIECE, channels), jnp.float32),
            pltpu.VMEM((WL, cols, THIRD * len(part.places), channels), jnp.bfloat16),
            pltpu.SemaphoreType.DMA((len(weights),)),
            pltpu.SemaphoreType.DMA,
        ],
        input_output_aliases=aliases,
        compiler_params=pltpu.CompilerParams(vmem_limit_bytes=VMEM_LIMIT),
        cost_estimate=pl.CostEstimate(flops=12_000_000_000, bytes_accessed=14_000_000, transcendentals=4_000_000),
    )(*operands)


def per_device(
    latent,
    attention_gain,
    triple_weight,
    head_scale,
    output_weight,
    feed_gain,
    up_weight,
    down_weight,
):
    x = latent.transpose(0, 2, 1, 3)
    levels, cols, rows, channels = x.shape
    head_dim = channels // head_scale.shape[0]
    pairs = levels // WL
    mid = rows // 2
    lat = lax.axis_index("lat")
    count = lax.axis_size("lat")
    seam = jnp.stack([lat == 0, lat == count - 1]).astype(jnp.float32)
    factor = head_scale * (LOG2E / head_dim ** 0.5)
    parts = [Part(half, rows) for half in (0, 1)]
    bias = seam_table()
    gains = [attention_gain.reshape(1, -1), feed_gain.reshape(1, -1)]
    weights = [triple_weight, output_weight, up_weight, down_weight]

    above = from_behind(x[:, :, rows - HALF_LAT:], "lat", 1)
    below = from_behind(x[:, :, :HALF_LAT], "lat", -1)
    edges = jnp.concatenate([above, below], axis=2)
    edge_left = from_behind(edges[:, HALF_LON:], "lon", 1)
    edge_right = from_behind(edges[:, :HALF_LON], "lon", -1)
    pad = ((0, 0), (0, 0), (0, TILE - 2 * HALF_LAT), (0, 0))
    edges = [jnp.pad(e, pad) for e in (edges, edge_left, edge_right)]

    out, previous = None, None
    pieces = []
    for p in range(pairs):
        for half in (0, 1):
            level, span = slice(WL * p, WL * p + WL), slice(half * mid, half * mid + mid)
            left, right = x[level, HALF_LON:, span], x[level, :HALF_LON, span]
            if previous is not None:
                left, right, *previous = lax.optimization_barrier((left, right, *previous))
            previous = [from_behind(left, "lon", 1), from_behind(right, "lon", -1)]
            pieces.append(previous)
    for p in range(pairs):
        local = pieces[2 * p:2 * p + 2]
        out, carry = block(parts[0], p, seam, factor, x, local, edges, bias, gains, None, weights, out)
        out = block(parts[1], p, seam, factor, x, local, edges, bias, gains, carry, weights, out)
    return out.transpose(0, 2, 1, 3)


def solution(mesh):
    in_specs = (P(None, "lat", "lon", None), P(), P(), P(), P(), P(), P(), P())
    out_specs = P(None, "lat", "lon", None)
    return jax.shard_map(
        per_device, mesh=mesh, in_specs=in_specs, out_specs=out_specs, check_vma=False
    )
```

time: 1000 us -> 178 us (0.18)
  matrix products: 438 us -> 0 us
  other arithmetic: 233 us -> 2.53 us
  local copies, waits for them, and re-layouts: 222 us -> 14.1 us
  Pallas kernels: 0 us -> 97.7 us
  waiting for transfers between devices: 92.3 us -> 25.4 us
  starting transfers between devices: 10.9 us -> 35.6 us
    dot_general x36 -> x0, matrix products: 438 us -> none  [the longest x16 156 us: one_band(): jnp.einsum('aehlrcmsf,amsefhd->alrechd', attn_probs, values_part, preferr...]
    reduce_sum x19 -> x0, other arithmetic: 214 us -> none  [the longest x16 204 us: one_band(): jnp.sum(weights, axis=-1, keepdims=True)]
    pallas_call x0 -> x4, Pallas kernels: none -> 97.7 us  [block(): pl.pallas_call(functools.partial(block_kernel, part, pair, out is not Non...]
    reshape x37 -> x0, local copies, waits for them, and re-layouts: 89.3 us -> none  [the longest x16 29.8 us: one_band(): band.reshape(level_wins, WL, WLAT, col_wins, WLON, 3, heads, head_dim)]
    ppermute x4 -> x12, waiting for transfers between devices: 92.3 us -> 25.4 us  [from_behind(): lax.ppermute(shard, axis, [(i, (i + by) % count) for i in range(count)])]
    slice x19 -> x2, local copies, waits for them, and re-layouts: 36.1 us -> 6.6 us  [the longest x1 4.54 us: per_device(): left, right = (x[level, HALF_LON:, span], x[level, :HALF_LON, span])]
    convert_element_type x18 -> x0, local copies, waits for them, and re-layouts: 25.4 us -> none  [the longest x2 19.3 us: per_device(): inputs.astype(jnp.float32)]
    ppermute x4 -> x12, starting transfers between devices: 10.9 us -> 35.6 us  [from_behind(): lax.ppermute(shard, axis, [(i, (i + by) % count) for i in range(count)])]
  transfers between devices with their start and end apart: 4 -> 12, of which waited for: 3 -> 4; matrix products, arithmetic and copies ran while one was open for 3% -> 3% of each run, Pallas kernels for 0% -> 41%
where the time goes in v2:
time: 178 us; the launch traced here: 176 us
  Pallas kernels  97.7 us (55%)
  starting transfers between devices  35.6 us (20%)
  waiting for transfers between devices  25.4 us (14%)
  local copies, waits for them, and re-layouts  14.1 us (8%)
  other arithmetic  2.53 us (1%)
    pallas_call x4, Pallas kernels, block(): pl.pallas_call(functools.partial(block_kernel, part, pair, out is not Non...  97.7 us
    ppermute x12, starting transfers between devices, from_behind(): lax.ppermute(shard, axis, [(i, (i + by) % count) for i in range(count)])  35.6 us
    ppermute x12, waiting for transfers between devices, from_behind(): lax.ppermute(shard, axis, [(i, (i + by) % count) for i in range(count)])  25.4 us
    unnamed x40, local copies, waits for them, and re-layouts  7.28 us
    slice x1, local copies, waits for them, and re-layouts, per_device(): left, right = (x[level, HALF_LON:, span], x[level, :HALF_LON, span])  4.54 us
  transfers between devices with their start and end apart: 12, of which 4 were waited for; matrix products, arithmetic and copies ran while one was open for 3% of the time, Pallas kernels for 41%

profile of v2, /device:TPU:1, one launch (start us, length us, event | category | flops | bytes accessed | tf_op | source)
XLA Modules:
  0.0 175.8 jit_solution(12297813280410542975)
XLA Ops:
  0.0 0.0 copy-start.19
  0.0 4.5 %fusion.3 = (bf16[2,6,48,512]{3,2,1,0:T(8,128)(2,1)}, bf16[2,6,48,512]{3,2,1,0:T(8,128)(2,1)}, bf16[2,6,48,512]{3,2,1,0:T(8,128)(2,1)}, bf16[2,6,48,512]{3,2,1,0...) fusion(bf16[4,12,96,512]{3,2,1,0:T(8,128)(2,1)} %bitcast.6), kind=kLoop, calls=%fused_computation.10 | loop fusion | bytes 9437184 | tf_op jit(solution)/shard_map/slice | solution.py:341
  4.6 0.0 copy-start.7
  4.6 0.0 copy-start.8
  4.6 0.0 copy-start.10
  4.6 9.1 %collective-permute-start.1 = (bf16[2,6,48,512]{3,2,1,0:T(8,128)(2,1)}, bf16[2,6,48,512]{3,2,1,0:T(8,128)(2,1)S(1)}, u32[]{:S(2)}, u32[]{:S(2)}) collective-permute-start(bf16[2,6,48,512]{3,2,1,0:T(8,128)(2,1)} %get-tuple-element.27), channel_id=1, source_target_pairs={{0,31},{1,0},{2,1},{3,2},{4,3},{5,4},{6,5},{7,6},{8,7},{9,8},{10,9... | collective-permute-start | bytes 1769480 | tf_op jit(solution)/shard_map/ppermute | solution.py:31
  13.7 0.0 collective-permute-start
  13.7 2.1 %fusion.2 = (bf16[4,12,3,512]{3,2,1,0:T(4,128)(2,1)}, bf16[4,12,3,512]{3,2,1,0:T(4,128)(2,1)}) fusion(bf16[4,12,96,512]{3,2,1,0:T(8,128)(2,1)} %bitcast.7), kind=kLoop, calls=%fused_computation.9 | loop fusion | bytes 589824 | tf_op jit(solution)/shard_map/slice | solution.py:328
  15.8 1.6 collective-permute-start.8
  17.4 0.0 collective-permute-start.9
  17.4 0.0 copy-done.19
  17.4 13.0 %collective-permute-done.8 = bf16[4,12,3,512]{3,2,1,0:T(4,128)(2,1)} collective-permute-done((bf16[4,12,3,512]{3,2,1,0:T(4,128)(2,1)}, bf16[4,12,3,512]{3,2,1,0:T(4,128)(2,1)}, u32[]{:S(2)}, u32[]{:S(2)}) %collective-permute-start.8) | collective-permute-done | bytes 147488 | tf_op jit(solution)/shard_map/ppermute | solution.py:31
  30.3 2.4 %collective-permute-done.9 = bf16[4,12,3,512]{3,2,1,0:T(4,128)(2,1)} collective-permute-done((bf16[4,12,3,512]{3,2,1,0:T(4,128)(2,1)}, bf16[4,12,3,512]{3,2,1,0:T(4,128)(2,1)}, u32[]{:S(2)}, u32[]{:S(2)}) %collective-permute-start.9) | collective-permute-done | bytes 147488 | tf_op jit(solution)/shard_map/ppermute | solution.py:31
  32.7 1.2 fusion.1
  33.9 3.1 %collective-permute-start.11 = (bf16[4,6,6,512]{3,2,1,0:T(8,128)(2,1)S(1)}, bf16[4,6,6,512]{3,2,1,0:T(8,128)(2,1)S(1)}, u32[]{:S(2)}, u32[]{:S(2)}) collective-permute-start(bf16[4,6,6,512]{3,2,1,0:T(8,128)(2,1)S(1)} %get-tuple-element.35), channel_id=1, source_target_pairs={{0,31},{1,0},{2,1},{3,2},{4,3},{5,4},{6,5},{7,6},{8,7},{9,8},{10,9... | collective-permute-start | bytes 442376 | tf_op jit(solution)/shard_map/ppermute | solution.py:31
  37.1 0.0 collective-permute-start.10
  37.1 0.1 add_convert_fusion.refs_0_
  37.2 1.2 pad_maximum_fusion
  38.4 0.1 pad.11.refs_5_
  38.5 2.5 %collective-permute-done.11 = bf16[4,6,6,512]{3,2,1,0:T(8,128)(2,1)S(1)} collective-permute-done((bf16[4,6,6,512]{3,2,1,0:T(8,128)(2,1)S(1)}, bf16[4,6,6,512]{3,2,1,0:T(8,128)(2,1)S(1)}, u32[]{:S(2)}, u32[]{:S(2)}) %collective-permute-start.11) | collective-permute-done | bytes 147488 | tf_op jit(solution)/shard_map/ppermute | solution.py:31
  41.0 7.6 %collective-permute-done.10 = bf16[4,6,6,512]{3,2,1,0:T(8,128)(2,1)S(1)} collective-permute-done((bf16[4,6,6,512]{3,2,1,0:T(8,128)(2,1)S(1)}, bf16[4,6,6,512]{3,2,1,0:T(8,128)(2,1)S(1)}, u32[]{:S(2)}, u32[]{:S(2)}) %collective-permute-start.10) | collective-permute-done | bytes 147488 | tf_op jit(solution)/shard_map/ppermute | solution.py:31
  48.6 0.0 collective-permute-done.1.refs_4_.refs_10_
  48.6 0.0 collective-permute-done.refs_3_.refs_9_
  48.6 0.1 collective-permute-start.2
  48.7 7.2 %collective-permute-start.3 = (bf16[2,6,48,512]{3,2,1,0:T(8,128)(2,1)}, bf16[2,6,48,512]{3,2,1,0:T(8,128)(2,1)S(1)}, u32[]{:S(2)}, u32[]{:S(2)}) collective-permute-start(bf16[2,6,48,512]{3,2,1,0:T(8,128)(2,1)} %get-tuple-element.16), channel_id=1, source_target_pairs={{0,31},{1,0},{2,1},{3,2},{4,3},{5,4},{6,5},{7,6},{8,7},{9,8},{10,9... | collective-permute-start | bytes 1769480 | tf_op jit(solution)/shard_map/ppermute | solution.py:31
  55.9 0.0 copy-done.1
  55.9 0.0 copy-done.6
  55.9 0.0 copy-done.7
  55.9 0.0 copy-done.8
  55.9 0.0 copy-done.10
  55.9 0.0 copy-start
  55.9 2.3 %copy-done = bf16[4,96,12,512]{3,1,2,0:T(8,128)(2,1)S(1)} copy-done((bf16[4,96,12,512]{3,1,2,0:T(8,128)(2,1)S(1)}, bf16[4,96,12,512]{3,1,2,0:T(8,128)(2,1)}, u32[]{:S(2)}) %copy-start) | copy-done | bytes 4718616
  58.3 1.6 copy-done.2
  59.9 1.4 copy-done.3
  61.3 1.0 copy-done.5
  62.3 0.8 copy-done.13
  63.1 0.0 copy-start.11
  63.2 0.0 copy-start.12
  63.2 0.0 copy-start.14
  63.2 22.7 %shard_map.145 = (bf16[4,12,96,512]{3,2,1,0:T(8,128)(2,1)}, f32[6,72,512]{2,1,0:T(8,128)S(1)}) custom-call(f32[2]{0:T(128)S(1)} %add_convert_fusion.refs_0_, f32[8]{0:T(128)S(1)} %broadcast_multiply_fusion.refs_1_, bf16[4,12,96,512]{3,2,1,0:T(8,128)(2,1)S(1)} %bitcast.8, bf16[2,6,48,512]{3,2,1,0:T(8,128)(2,1)S(1)} %collective-permute-done.refs_3_.refs_9_, ...), custom_call_target="tpu_custom_call" | custom-call | flops 12000000000 | bytes 14000000 | tf_op jit(solution)/shard_map/pallas_call | solution.py:282
  85.9 0.0 collective-permute-done.2.refs_3_
  85.9 0.0 collective-permute-done.3.refs_4_
  85.9 0.0 copy-done.18
  85.9 0.1 collective-permute-start.4
  86.0 0.0 copy-done.17
  86.0 7.2 %collective-permute-start.5 = (bf16[2,6,48,512]{3,2,1,0:T(8,128)(2,1)S(1)}, bf16[2,6,48,512]{3,2,1,0:T(8,128)(2,1)S(1)}, u32[]{:S(2)}, u32[]{:S(2)}) collective-permute-start(bf16[2,6,48,512]{3,2,1,0:T(8,128)(2,1)S(1)} %copy-done.17), channel_id=1, source_target_pairs={{0,31},{1,0},{2,1},{3,2},{4,3},{5,4},{6,5},{7,6},{8,7},{9,8},{10,9... | collective-permute-start | bytes 1769480 | tf_op jit(solution)/shard_map/ppermute | solution.py:31
  93.1 0.0 copy-done.4
  93.1 0.0 copy-done.9
  93.2 0.0 copy-done.11
  93.2 0.0 copy-done.12
  93.2 0.0 copy-done.14
  93.2 0.0 copy-start.16
  93.2 0.0 copy-start.15
  93.2 26.1 %shard_map.146.refs_17_ = bf16[4,12,96,512]{3,2,1,0:T(8,128)(2,1)} custom-call(f32[2]{0:T(128)S(1)} %add_convert_fusion.refs_0_, f32[8]{0:T(128)S(1)} %broadcast_multiply_fusion.refs_1_, bf16[4,12,96,512]{3,2,1,0:T(8,128)(2,1)S(1)} %bitcast.9, bf16[2,6,48,512]{3,2,1,0:T(8,128)(2,1)S(1)} %collective-permute-done.2.refs_3_, ...), custom_call_target="tpu_custom_call", output_to_operand_aliasing={{}: (23, {})} | custom-call | flops 12000000000 | bytes 14000000 | tf_op jit(solution)/shard_map/pallas_call | solution.py:282
  119.3 0.0 collective-permute-done.4.refs_3_.refs_9_
  119.3 0.0 collective-permute-done.5.refs_4_.refs_10_
  119.3 0.0 copy-done.16
  119.3 0.1 collective-permute-start.6
  119.4 0.0 copy-done.15
  119.4 7.2 %collective-permute-start.7 = (bf16[2,6,48,512]{3,2,1,0:T(8,128)(2,1)S(1)}, bf16[2,6,48,512]{3,2,1,0:T(8,128)(2,1)S(1)}, u32[]{:S(2)}, u32[]{:S(2)}) collective-permute-start(bf16[2,6,48,512]{3,2,1,0:T(8,128)(2,1)S(1)} %copy-done.15), channel_id=1, source_target_pairs={{0,31},{1,0},{2,1},{3,2},{4,3},{5,4},{6,5},{7,6},{8,7},{9,8},{10,9... | collective-permute-start | bytes 1769480 | tf_op jit(solution)/shard_map/ppermute | solution.py:31
  126.6 22.6 %shard_map.147 = (bf16[4,12,96,512]{3,2,1,0:T(8,128)(2,1)}, f32[6,72,512]{2,1,0:T(8,128)S(1)}) custom-call(f32[2]{0:T(128)S(1)} %add_convert_fusion.refs_0_, f32[8]{0:T(128)S(1)} %broadcast_multiply_fusion.refs_1_, bf16[4,12,96,512]{3,2,1,0:T(8,128)(2,1)S(1)} %bitcast.11, ...), custom_call_target="tpu_custom_call", output_to_operand_aliasing={{0}: (17, {})} | custom-call | flops 12000000000 | bytes 14000000 | tf_op jit(solution)/shard_map/pallas_call | solution.py:282
  149.2 0.0 collective-permute-done.6.refs_3_
  149.2 0.0 collective-permute-done.7.refs_4_
  149.3 26.3 %shard_map.148 = bf16[4,12,96,512]{3,2,1,0:T(8,128)(2,1)} custom-call(f32[2]{0:T(128)S(1)} %add_convert_fusion.refs_0_, f32[8]{0:T(128)S(1)} %broadcast_multiply_fusion.refs_1_, bf16[4,12,96,512]{3,2,1,0:T(8,128)(2,1)S(1)} %bitcast.12, bf16[2,6,48,512]{3,2,1,0:T(8,128)(2,1)S(1)} %collective-permute-done.6.refs_3_, ...), custom_call_target="tpu_custom_call", output_to_operand_aliasing={{}: (23, {})} | custom-call | flops 12000000000 | bytes 14000000 | tf_op jit(solution)/shard_map/pallas_call | solution.py:282
  (13 shorter events, 0.1 us)
Async XLA Ops:
  0.0 17.4 %copy-start.19 = (f32[8]{0:T(128)S(1)}, f32[8]{0:T(128)}, u32[]{:S(2)}) copy-start(f32[8]{0:T(128)} %param.18) | copy-start | bytes 100
  4.5 51.4 %copy-start.1 = (bf16[512,2048]{1,0:T(8,128)(2,1)S(1)}, bf16[512,2048]{1,0:T(8,128)(2,1)}, u32[]{:S(2)}) copy-start(bf16[512,2048]{1,0:T(8,128)(2,1)} %refs_21_.3) | copy-start | bytes 6291460
  4.5 51.4 %copy-start.6 = (f32[512]{0:T(512)S(1)}, f32[512]{0:T(512)}, u32[]{:S(2)}) copy-start(f32[512]{0:T(512)} %param.16) | copy-start | bytes 6148
  4.6 51.3 %copy-start.7 = (f32[512]{0:T(512)S(1)}, f32[512]{0:T(512)}, u32[]{:S(2)}) copy-start(f32[512]{0:T(512)} %param.20) | copy-start | bytes 6148
  4.6 51.3 %copy-start.8 = (f32[144,144]{1,0:T(8,128)S(1)}, f32[144,144]{1,0:T(8,128)}, u32[]{:S(2)}) copy-start(f32[144,144]{1,0:T(8,128)} %constant.34.clone.refs_10_.refs_15_) | copy-start | bytes 248836
  4.6 51.3 %copy-start.10 = (bf16[192,256]{1,0:T(8,128)(2,1)S(1)}, bf16[192,256]{1,0:T(8,128)(2,1)}, u32[]{:S(2)}) copy-start(bf16[192,256]{1,0:T(8,128)(2,1)} %constant.28.clone.refs_8_) | copy-start | bytes 294916
  4.6 44.0 %collective-permute-start.1 = (bf16[2,6,48,512]{3,2,1,0:T(8,128)(2,1)}, bf16[2,6,48,512]{3,2,1,0:T(8,128)(2,1)S(1)}, u32[]{:S(2)}, u32[]{:S(2)}) collective-permute-start(bf16[2,6,48,512]{3,2,1,0:T(8,128)(2,1)} %get-tuple-element.27), channel_id=1, source_target_pairs={{0,31},{1,0},{2,1},{3,2},{4,3},{5,4},{6,5},{7,6},{8,7},{9,8},{10,9... | collective-permute-start | bytes 1769480 | tf_op jit(solution)/shard_map/ppermute | solution.py:31
  13.7 34.9 %collective-permute-start = (bf16[2,6,48,512]{3,2,1,0:T(8,128)(2,1)}, bf16[2,6,48,512]{3,2,1,0:T(8,128)(2,1)S(1)}, u32[]{:S(2)}, u32[]{:S(2)}) collective-permute-start(bf16[2,6,48,512]{3,2,1,0:T(8,128)(2,1)} %get-tuple-element.28), channel_id=1, source_target_pairs={{0,1},{1,2},{2,3},{3,4},{4,5},{5,6},{6,7},{7,8},{8,9},{9,10},{10,1... | collective-permute-start | bytes 1769480 | tf_op jit(solution)/shard_map/ppermute | solution.py:31
  15.8 14.6 %collective-permute-start.8 = (bf16[4,12,3,512]{3,2,1,0:T(4,128)(2,1)}, bf16[4,12,3,512]{3,2,1,0:T(4,128)(2,1)}, u32[]{:S(2)}, u32[]{:S(2)}) collective-permute-start(bf16[4,12,3,512]{3,2,1,0:T(4,128)(2,1)} %get-tuple-element.25), channel_id=1, source_target_pairs={{0,32},{32,64},{64,96},{96,0},{1,33},{33,65},{65,97},{97,1},{2,34}... | collective-permute-start | bytes 442376 | tf_op jit(solution)/shard_map/ppermute | solution.py:31
  17.4 15.3 %collective-permute-start.9 = (bf16[4,12,3,512]{3,2,1,0:T(4,128)(2,1)}, bf16[4,12,3,512]{3,2,1,0:T(4,128)(2,1)}, u32[]{:S(2)}, u32[]{:S(2)}) collective-permute-start(bf16[4,12,3,512]{3,2,1,0:T(4,128)(2,1)} %get-tuple-element.26), channel_id=1, source_target_pairs={{0,96},{32,0},{64,32},{96,64},{1,97},{33,1},{65,33},{97,65},{2,98}... | collective-permute-start | bytes 442376 | tf_op jit(solution)/shard_map/ppermute | solution.py:31
  33.9 7.0 %collective-permute-start.11 = (bf16[4,6,6,512]{3,2,1,0:T(8,128)(2,1)S(1)}, bf16[4,6,6,512]{3,2,1,0:T(8,128)(2,1)S(1)}, u32[]{:S(2)}, u32[]{:S(2)}) collective-permute-start(bf16[4,6,6,512]{3,2,1,0:T(8,128)(2,1)S(1)} %get-tuple-element.35), channel_id=1, source_target_pairs={{0,31},{1,0},{2,1},{3,2},{4,3},{5,4},{6,5},{7,6},{8,7},{9,8},{10,9... | collective-permute-start | bytes 442376 | tf_op jit(solution)/shard_map/ppermute | solution.py:31
  37.1 11.5 %collective-permute-start.10 = (bf16[4,6,6,512]{3,2,1,0:T(8,128)(2,1)S(1)}, bf16[4,6,6,512]{3,2,1,0:T(8,128)(2,1)S(1)}, u32[]{:S(2)}, u32[]{:S(2)}) collective-permute-start(bf16[4,6,6,512]{3,2,1,0:T(8,128)(2,1)S(1)} %get-tuple-element.36), channel_id=1, source_target_pairs={{0,1},{1,2},{2,3},{3,4},{4,5},{5,6},{6,7},{7,8},{8,9},{9,10},{10,1... | collective-permute-start | bytes 442376 | tf_op jit(solution)/shard_map/ppermute | solution.py:31
  48.6 37.2 %collective-permute-start.2 = (bf16[2,6,48,512]{3,2,1,0:T(8,128)(2,1)}, bf16[2,6,48,512]{3,2,1,0:T(8,128)(2,1)S(1)}, u32[]{:S(2)}, u32[]{:S(2)}) collective-permute-start(bf16[2,6,48,512]{3,2,1,0:T(8,128)(2,1)} %get-tuple-element.15), channel_id=1, source_target_pairs={{0,1},{1,2},{2,3},{3,4},{4,5},{5,6},{6,7},{7,8},{8,9},{9,10},{10,1... | collective-permute-start | bytes 1769480 | tf_op jit(solution)/shard_map/ppermute | solution.py:31
  48.7 37.1 %collective-permute-start.3 = (bf16[2,6,48,512]{3,2,1,0:T(8,128)(2,1)}, bf16[2,6,48,512]{3,2,1,0:T(8,128)(2,1)S(1)}, u32[]{:S(2)}, u32[]{:S(2)}) collective-permute-start(bf16[2,6,48,512]{3,2,1,0:T(8,128)(2,1)} %get-tuple-element.16), channel_id=1, source_target_pairs={{0,31},{1,0},{2,1},{3,2},{4,3},{5,4},{6,5},{7,6},{8,7},{9,8},{10,9... | collective-permute-start | bytes 1769480 | tf_op jit(solution)/shard_map/ppermute | solution.py:31
  55.9 2.3 %copy-start = (bf16[4,96,12,512]{3,1,2,0:T(8,128)(2,1)S(1)}, bf16[4,96,12,512]{3,1,2,0:T(8,128)(2,1)}, u32[]{:S(2)}) copy-start(bf16[4,96,12,512]{3,1,2,0:T(8,128)(2,1)} %param.15) | copy-start | bytes 14155780
  58.3 1.6 copy-start.2
  59.8 1.4 copy-start.3
  61.3 1.0 copy-start.5
  62.3 0.8 copy-start.13
  63.1 22.7 %copy-start.18 = (bf16[2,6,48,512]{3,2,1,0:T(8,128)(2,1)S(1)}, bf16[2,6,48,512]{3,2,1,0:T(8,128)(2,1)}, u32[]{:S(2)}) copy-start(bf16[2,6,48,512]{3,2,1,0:T(8,128)(2,1)} %get-tuple-element.17) | copy-start | bytes 1769476
  63.1 22.8 %copy-start.17 = (bf16[2,6,48,512]{3,2,1,0:T(8,128)(2,1)S(1)}, bf16[2,6,48,512]{3,2,1,0:T(8,128)(2,1)}, u32[]{:S(2)}) copy-start(bf16[2,6,48,512]{3,2,1,0:T(8,128)(2,1)} %get-tuple-element.18) | copy-start | bytes 1769476
  63.1 30.0 %copy-start.4 = (bf16[512,1536]{1,0:T(8,128)(2,1)S(1)}, bf16[512,1536]{1,0:T(8,128)(2,1)}, u32[]{:S(2)}) copy-start(bf16[512,1536]{1,0:T(8,128)(2,1)} %refs_19_.3) | copy-start | bytes 4718596
  63.1 30.0 %copy-start.9 = (bf16[192,256]{1,0:T(8,128)(2,1)S(1)}, bf16[192,256]{1,0:T(8,128)(2,1)}, u32[]{:S(2)}) copy-start(bf16[192,256]{1,0:T(8,128)(2,1)} %constant.30.clone.refs_11_) | copy-start | bytes 294916
  63.1 30.0 %copy-start.11 = (bf16[128,144]{1,0:T(8,128)(2,1)S(1)}, bf16[128,144]{1,0:T(8,128)(2,1)}, u32[]{:S(2)}) copy-start(bf16[128,144]{1,0:T(8,128)(2,1)} %constant.33.clone.refs_14_) | copy-start | bytes 110596
  63.2 30.0 %copy-start.12 = (bf16[128,168]{1,0:T(8,128)(2,1)S(1)}, bf16[128,168]{1,0:T(8,128)(2,1)}, u32[]{:S(2)}) copy-start(bf16[128,168]{1,0:T(8,128)(2,1)} %constant.32.clone.refs_13_) | copy-start | bytes 129028
  63.2 30.0 %copy-start.14 = (bf16[24,128]{1,0:T(8,128)(2,1)S(1)}, bf16[24,128]{1,0:T(8,128)(2,1)}, u32[]{:S(2)}) copy-start(bf16[24,128]{1,0:T(8,128)(2,1)} %constant.31.clone.refs_12_) | copy-start | bytes 18436
  85.9 33.4 %collective-permute-start.4 = (bf16[2,6,48,512]{3,2,1,0:T(8,128)(2,1)S(1)}, bf16[2,6,48,512]{3,2,1,0:T(8,128)(2,1)S(1)}, u32[]{:S(2)}, u32[]{:S(2)}) collective-permute-start(bf16[2,6,48,512]{3,2,1,0:T(8,128)(2,1)S(1)} %copy-done.18), channel_id=1, source_target_pairs={{0,1},{1,2},{2,3},{3,4},{4,5},{5,6},{6,7},{7,8},{8,9},{9,10},{10,1... | collective-permute-start | bytes 1769480 | tf_op jit(solution)/shard_map/ppermute | solution.py:31
  86.0 33.3 %collective-permute-start.5 = (bf16[2,6,48,512]{3,2,1,0:T(8,128)(2,1)S(1)}, bf16[2,6,48,512]{3,2,1,0:T(8,128)(2,1)S(1)}, u32[]{:S(2)}, u32[]{:S(2)}) collective-permute-start(bf16[2,6,48,512]{3,2,1,0:T(8,128)(2,1)S(1)} %copy-done.17), channel_id=1, source_target_pairs={{0,31},{1,0},{2,1},{3,2},{4,3},{5,4},{6,5},{7,6},{8,7},{9,8},{10,9... | collective-permute-start | bytes 1769480 | tf_op jit(solution)/shard_map/ppermute | solution.py:31
  93.2 26.1 %copy-start.16 = (bf16[2,6,48,512]{3,2,1,0:T(8,128)(2,1)S(1)}, bf16[2,6,48,512]{3,2,1,0:T(8,128)(2,1)}, u32[]{:S(2)}) copy-start(bf16[2,6,48,512]{3,2,1,0:T(8,128)(2,1)} %get-tuple-element.19) | copy-start | bytes 1769476
  93.2 26.2 %copy-start.15 = (bf16[2,6,48,512]{3,2,1,0:T(8,128)(2,1)S(1)}, bf16[2,6,48,512]{3,2,1,0:T(8,128)(2,1)}, u32[]{:S(2)}) copy-start(bf16[2,6,48,512]{3,2,1,0:T(8,128)(2,1)} %get-tuple-element.20) | copy-start | bytes 1769476
  119.3 29.9 %collective-permute-start.6 = (bf16[2,6,48,512]{3,2,1,0:T(8,128)(2,1)S(1)}, bf16[2,6,48,512]{3,2,1,0:T(8,128)(2,1)S(1)}, u32[]{:S(2)}, u32[]{:S(2)}) collective-permute-start(bf16[2,6,48,512]{3,2,1,0:T(8,128)(2,1)S(1)} %copy-done.16), channel_id=1, source_target_pairs={{0,1},{1,2},{2,3},{3,4},{4,5},{5,6},{6,7},{7,8},{8,9},{9,10},{10,1... | collective-permute-start | bytes 1769480 | tf_op jit(solution)/shard_map/ppermute | solution.py:31
  119.4 29.8 %collective-permute-start.7 = (bf16[2,6,48,512]{3,2,1,0:T(8,128)(2,1)S(1)}, bf16[2,6,48,512]{3,2,1,0:T(8,128)(2,1)S(1)}, u32[]{:S(2)}, u32[]{:S(2)}) collective-permute-start(bf16[2,6,48,512]{3,2,1,0:T(8,128)(2,1)S(1)} %copy-done.15), channel_id=1, source_target_pairs={{0,31},{1,0},{2,1},{3,2},{4,3},{5,4},{6,5},{7,6},{8,7},{9,8},{10,9... | collective-permute-start | bytes 1769480 | tf_op jit(solution)/shard_map/ppermute | solution.py:31

commit v3 on v2

v3 whole, which is shorter than its diff:
```python
import functools

import jax
import jax.numpy as jnp
import numpy as np
from jax import lax
from jax.experimental import pallas as pl
from jax.experimental.pallas import tpu as pltpu
from jax.sharding import PartitionSpec as P

WL = 2
WLAT = 6
WLON = 12
HALF_LAT = WLAT // 2
HALF_LON = WLON // 2
EPS = 1e-05
SLABS = 4
PIECE = SLABS * WLAT
SIDE_SLABS = WL * HALF_LON
SIDE = SIDE_SLABS * WLAT
TOKENS = 2 * SIDE
GROUPS = SIDE_SLABS // SLABS
TILE = 16
THIRD = 32
LOG2E = 1.4426950408889634
VMEM_LIMIT = 44 * 1024 * 1024


def from_behind(shard, axis, by):
    count = lax.axis_size(axis)
    return lax.ppermute(shard, axis, [(i, (i + by) % count) for i in range(count)])


def norm_rows(values, gain):
    average = jnp.mean(values, axis=-1, keepdims=True)
    centred = values - average
    spread = jnp.mean(centred * centred, axis=-1, keepdims=True)
    return centred * lax.rsqrt(spread + EPS) * gain


def gelu(x):
    half = 0.5 * x
    return half + half * lax.erf(x * 0.7071067811865476)


class Plan:
    def __init__(self, rows):
        self.rows = rows
        self.count = rows // WLAT + 1
        half = rows // 2
        cut = self.count // 2
        edge = ("edge", 0, 0)
        self.picks = [
            (range(cut), [("main", 0, half), edge]),
            (range(cut, self.count - 1), [("main", half - TILE, rows)]),
            (range(self.count - 1, self.count), [("main", rows - TILE, rows), edge]),
        ]
        self.places = [(r, r + THIRD) for r in range(0, rows, THIRD)]
        self.tables = [self.pick_table(*p) for p in self.picks] + [self.place_table(*p) for p in self.places]

    def bands_of(self, r0, r1):
        return (r0 + HALF_LAT) // WLAT, (r1 - 1 + HALF_LAT) // WLAT + 1

    def pick_table(self, bands, segments):
        width = sum(SLABS * (r1 - r0 if name != "edge" else TILE) for name, r0, r1 in segments)
        table = np.zeros((len(bands) * PIECE, width), np.float32)
        for n, band in enumerate(bands):
            for s in range(SLABS):
                for i in range(WLAT):
                    r = band * WLAT - HALF_LAT + i
                    start = 0
                    for name, r0, r1 in segments:
                        span = TILE if name == "edge" else r1 - r0
                        if name != "edge" and r0 <= r < r1:
                            table[n * PIECE + s * WLAT + i, start + s * span + r - r0] = 1
                        elif name == "edge" and r < 0:
                            table[n * PIECE + s * WLAT + i, start + s * span + r + HALF_LAT] = 1
                        elif name == "edge" and r >= self.rows:
                            table[n * PIECE + s * WLAT + i, start + s * span + r - self.rows + TILE // 2] = 1
                        start += SLABS * span
        return jnp.asarray(table, jnp.bfloat16)

    def place_table(self, r0, r1):
        b0, b1 = self.bands_of(r0, r1)
        table = np.zeros((SLABS * (r1 - r0), (b1 - b0) * PIECE), np.float32)
        for s in range(SLABS):
            for r in range(r0, r1):
                band, i = divmod(r + HALF_LAT, WLAT)
                table[s * (r1 - r0) + r - r0, (band - b0) * PIECE + s * WLAT + i] = 1
        return jnp.asarray(table, jnp.bfloat16)


def seam_table():
    i = np.arange(TOKENS) % WLAT < HALF_LAT
    return jnp.asarray(np.where(i[:, None] == i[None, :], 0.0, -1e30), jnp.float32)


def block_kernel(plan, pair, aliased, *refs):
    refs = list(refs)
    pop = lambda: refs.pop(0)
    seam_ref, factor_ref = pop(), pop()
    own_ref, around_refs, edge_ref = pop(), (pop(), pop()), pop()
    pick_refs = [pop() for _ in plan.picks]
    place_refs = [pop() for _ in plan.places]
    bias_ref, gain_ref, gain2_ref = pop(), pop(), pop()
    weights_hbm = [pop() for _ in range(4)]
    if aliased:
        pop()
    out_ref = pop()
    weights = [pop() for _ in range(4)]
    xw_ref, hw_ref, att_ref, yw_ref, ow_ref, wsem, osem = refs
    qkv_ref, wo_ref, up_ref, down_ref = weights
    channels = xw_ref.shape[-1]
    heads = factor_ref.shape[0]
    head_dim = channels // heads
    group_heads = 256 // head_dim
    count = plan.count

    copies = [pltpu.make_async_copy(a, b, wsem.at[i]) for i, (a, b) in enumerate(zip(weights_hbm, weights))]
    for copy in copies:
        copy.start()

    for dest, side in ((xw_ref, 0), (xw_ref, 1), (hw_ref, 0), (hw_ref, 1)):
        own = dest is xw_ref

        def rows_of(name, s, r0, r1):
            level, col = s // HALF_LON, s % HALF_LON + (side * HALF_LON if own else 0)
            if name == "edge":
                return edge_ref[level, col] if own else around_refs[side][level, col, plan.rows:plan.rows + TILE, :]
            ref = own_ref if own else around_refs[side]
            return ref[level, col, r0:r1, :]

        for g in range(GROUPS):
            ids = range(g * SLABS, (g + 1) * SLABS)
            at = (side * GROUPS + g) * PIECE
            for table, (bands, segments) in zip(pick_refs, plan.picks):
                stacked = jnp.concatenate([rows_of(n, s, r0, r1) for n, r0, r1 in segments for s in ids], axis=0)
                picked = jnp.dot(table[...], stacked, preferred_element_type=jnp.float32)
                for n, band in enumerate(bands):
                    dest[band, at:at + PIECE, :] = picked[n * PIECE:(n + 1) * PIECE]

    lane = lax.broadcasted_iota(jnp.int32, (1, 256), 1) // head_dim
    gain, gain2 = gain_ref[...], gain2_ref[...]
    copies[0].wait()

    def attend(b, bias):
        normed = norm_rows(xw_ref[b], gain).astype(jnp.bfloat16)
        around = norm_rows(hw_ref[b], gain).astype(jnp.bfloat16)
        mine = jnp.dot(normed, qkv_ref[...], preferred_element_type=jnp.float32)
        other = jnp.dot(around, qkv_ref[:, channels:], preferred_element_type=jnp.float32)
        for g in range(heads // group_heads):
            at = g * 256
            mixed = []
            for side in (0, 1):
                rows = slice(side * SIDE, (side + 1) * SIDE)
                q = mine[rows, at:at + 256]
                k, v = [
                    jnp.concatenate(
                        [mine[rows, c * channels + at:c * channels + at + 256],
                         other[rows, (c - 1) * channels + at:(c - 1) * channels + at + 256]], axis=0
                    ).astype(jnp.bfloat16)
                    for c in (1, 2)
                ]
                stacked = jnp.concatenate([jnp.where(lane == h, q, 0.0) for h in range(group_heads)], axis=0)
                scores = lax.dot_general(
                    stacked.astype(jnp.bfloat16), k, (((1,), (1,)), ((), ())), preferred_element_type=jnp.float32
                )
                probs = []
                for h in range(group_heads):
                    s = scores[h * SIDE:(h + 1) * SIDE]
                    if bias is not None:
                        s = s + bias[:SIDE]
                    top = jnp.max(s, axis=-1, keepdims=True)
                    e = jnp.exp2((s - top) * factor_ref[g * group_heads + h])
                    probs.append(e * (1.0 / jnp.sum(e, axis=-1, keepdims=True)))
                probs = jnp.concatenate(probs, axis=0).astype(jnp.bfloat16)
                out = jnp.dot(probs, v, preferred_element_type=jnp.float32)
                total = out[:SIDE]
                for h in range(1, group_heads):
                    total = jnp.where(lane == h, out[h * SIDE:(h + 1) * SIDE], total)
                mixed.append(total)
            att_ref[b, :, at:at + 256] = jnp.concatenate(mixed, axis=0).astype(jnp.bfloat16)

    def feed(b):
        residual = xw_ref[b] + jnp.dot(att_ref[b], wo_ref[...], preferred_element_type=jnp.float32)
        normed = norm_rows(residual, gain2).astype(jnp.bfloat16)
        acts = gelu(jnp.dot(normed, up_ref[...], preferred_element_type=jnp.float32)).astype(jnp.bfloat16)
        result = residual + jnp.dot(acts, down_ref[...], preferred_element_type=jnp.float32)
        at = b * PIECE
        at = at if isinstance(b, int) else pl.multiple_of(at, 8)
        for g in range(2 * GROUPS):
            yw_ref[g, pl.ds(at, PIECE), :] = result[g * PIECE:(g + 1) * PIECE]

    attend(0, bias_ref[...] * seam_ref[0])
    for copy in copies[1:]:
        copy.wait()

    def step(b, carry):
        feed(b - 1)
        attend(b, None)
        return carry

    lax.fori_loop(1, count - 1, step, 0)
    feed(count - 2)
    attend(count - 1, bias_ref[...] * seam_ref[1])
    feed(count - 1)

    for table, (r0, r1) in zip(place_refs, plan.places):
        b0, b1 = plan.bands_of(r0, r1)
        for g in range(2 * GROUPS):
            band_rows = yw_ref[g, b0 * PIECE:b1 * PIECE, :].astype(jnp.bfloat16)
            placed = jnp.dot(table[...], band_rows, preferred_element_type=jnp.float32).astype(jnp.bfloat16)
            for n in range(SLABS):
                s = g % GROUPS * SLABS + n
                col = s % HALF_LON + g // GROUPS * HALF_LON
                ow_ref[s // HALF_LON, col, r0:r1, :] = placed[n * THIRD:(n + 1) * THIRD]
    copy = pltpu.make_async_copy(ow_ref, out_ref.at[pl.ds(WL * pair, WL)], osem)
    copy.start()
    copy.wait()


def block(plan, pair, seam, factor, x, around, edges, bias, gains, weights, out):
    levels, cols, rows, channels = x.shape
    once = pl.Buffered(1)
    whole = lambda a: pl.BlockSpec(a.shape, lambda i, n=a.ndim: (0,) * n, pipeline_mode=once)
    smem = pl.BlockSpec(memory_space=pltpu.SMEM)
    hbm = pl.BlockSpec(memory_space=pl.ANY)
    mine = lambda r: pl.BlockSpec((WL, cols, r, channels), lambda i: (pair, 0, 0, 0), pipeline_mode=once)
    small = [*plan.tables, bias, *gains]
    operands = [seam, factor, x, *around, edges, *small, *weights]
    specs = [smem, smem, mine(rows), whole(around[0]), whole(around[1]), mine(TILE)]
    specs += [whole(a) for a in small] + [hbm] * len(weights)
    aliases = {}
    if out is not None:
        aliases = {len(operands): 0}
        operands.append(out)
        specs.append(hbm)
    return pl.pallas_call(
        functools.partial(block_kernel, plan, pair, out is not None),
        grid=(1,),
        out_shape=jax.ShapeDtypeStruct(x.shape, jnp.bfloat16),
        in_specs=specs,
        out_specs=hbm,
        scratch_shapes=[pltpu.VMEM(w.shape, w.dtype) for w in weights]
        + [
            pltpu.VMEM((plan.count, TOKENS, channels), jnp.float32),
            pltpu.VMEM((plan.count, TOKENS, channels), jnp.float32),
            pltpu.VMEM((plan.count, TOKENS, channels), jnp.bfloat16),
            pltpu.VMEM((2 * GROUPS, plan.count * PIECE, channels), jnp.float32),
            pltpu.VMEM((WL, cols, rows, channels), jnp.bfloat16),
            pltpu.SemaphoreType.DMA((len(weights),)),
            pltpu.SemaphoreType.DMA,
        ],
        input_output_aliases=aliases,
        compiler_params=pltpu.CompilerParams(vmem_limit_bytes=VMEM_LIMIT),
        cost_estimate=pl.CostEstimate(flops=24_000_000_000, bytes_accessed=20_000_000, transcendentals=8_000_000),
    )(*operands)


def per_device(
    latent,
    attention_gain,
    triple_weight,
    head_scale,
    output_weight,
    feed_gain,
    up_weight,
    down_weight,
):
    x = latent.transpose(0, 2, 1, 3)
    levels, cols, rows, channels = x.shape
    head_dim = channels // head_scale.shape[0]
    pairs = levels // WL
    lat = lax.axis_index("lat")
    count = lax.axis_size("lat")
    seam = jnp.stack([lat == 0, lat == count - 1]).astype(jnp.float32)
    factor = head_scale * (LOG2E / head_dim ** 0.5)
    plan = Plan(rows)
    bias = seam_table()
    gains = [attention_gain.reshape(1, -1), feed_gain.reshape(1, -1)]
    weights = [triple_weight, output_weight, up_weight, down_weight]

    above = from_behind(x[:, :, rows - HALF_LAT:], "lat", 1)
    below = from_behind(x[:, :, :HALF_LAT], "lat", -1)
    gap = ((0, 0), (0, 0), (0, TILE // 2 - HALF_LAT), (0, 0))
    edges = jnp.concatenate([jnp.pad(above, gap), jnp.pad(below, gap)], axis=2)

    out = None
    around = []
    for p in range(pairs):
        level = slice(WL * p, WL * p + WL)
        left, right = [
            jnp.concatenate([x[level, c], edges[level, c]], axis=2) for c in (slice(HALF_LON, cols), slice(0, HALF_LON))
        ]
        if p > 0:
            left, right, *around[-1] = lax.optimization_barrier((left, right, *around[-1]))
        around.append([from_behind(left, "lon", 1), from_behind(right, "lon", -1)])
    for p in range(pairs):
        out = block(plan, p, seam, factor, x, around[p], edges, bias, gains, weights, out)
    return out.transpose(0, 2, 1, 3)


def solution(mesh):
    in_specs = (P(None, "lat", "lon", None), P(), P(), P(), P(), P(), P(), P())
    out_specs = P(None, "lat", "lon", None)
    return jax.shard_map(
        per_device, mesh=mesh, in_specs=in_specs, out_specs=out_specs, check_vma=False
    )
```

time: 178 us -> 154 us (0.87); the launches traced: 176 us -> 154 us
  starting transfers between devices: 35.6 us -> 19.2 us
  local copies, waits for them, and re-layouts: 14.1 us -> 5.94 us
  waiting for transfers between devices: 25.4 us -> 29.4 us
  Pallas kernels: 97.7 us -> 94.9 us
  other arithmetic: 2.53 us -> 4.39 us
    ppermute x12 -> x6, starting transfers between devices: 35.6 us -> 19.2 us  [from_behind(): lax.ppermute(shard, axis, [(i, (i + by) % count) for i in range(count)])]
    unnamed x40 -> x28, local copies, waits for them, and re-layouts: 7.28 us -> 0.08 us
    ppermute x12 -> x6, waiting for transfers between devices: 25.4 us -> 29.4 us  [from_behind(): lax.ppermute(shard, axis, [(i, (i + by) % count) for i in range(count)])]
    pallas_call x4 -> x2, Pallas kernels: 97.7 us -> 94.9 us  [block(): pl.pallas_call(functools.partial(block_kernel, plan, pair, out is not Non...]
    concatenate x2 -> x4, other arithmetic: 2.45 us -> 4.31 us  [the longest x3 4.13 us: per_device(): jnp.concatenate([x[level, c], edges[level, c]], axis=2)]
    slice x1 -> x2, local copies, waits for them, and re-layouts: 4.54 us -> 4.58 us  [the longest x1 3.75 us: per_device(): x[level, c]]
  transfers between devices with their start and end apart: 12 -> 6, of which waited for: 4 -> 4; matrix products, arithmetic and copies ran while one was open for 3% -> 4% of each run, Pallas kernels for 41% -> 31%
where the time goes in v3:
time: 154 us
  Pallas kernels  94.9 us (62%)
  waiting for transfers between devices  29.4 us (19%)
  starting transfers between devices  19.2 us (12%)
  local copies, waits for them, and re-layouts  5.94 us (4%)
  other arithmetic  4.39 us (3%)
    pallas_call x2, Pallas kernels, block(): pl.pallas_call(functools.partial(block_kernel, plan, pair, out is not Non...  94.9 us
    ppermute x6, waiting for transfers between devices, from_behind(): lax.ppermute(shard, axis, [(i, (i + by) % count) for i in range(count)])  29.4 us
    ppermute x6, starting transfers between devices, from_behind(): lax.ppermute(shard, axis, [(i, (i + by) % count) for i in range(count)])  19.2 us
    concatenate x3, other arithmetic, per_device(): jnp.concatenate([x[level, c], edges[level, c]], axis=2)  4.13 us
    slice x1, local copies, waits for them, and re-layouts, per_device(): x[level, c]  3.75 us
  transfers between devices with their start and end apart: 6, of which 4 were waited for; matrix products, arithmetic and copies ran while one was open for 4% of the time, Pallas kernels for 31%

profile of v3, /device:TPU:1, one launch (start us, length us, event | category | flops | bytes accessed | tf_op | source)
XLA Modules:
  0.0 154.1 jit_solution(15801540197692436506)
XLA Ops:
  0.0 1.3 fusion.4
  1.3 3.1 %collective-permute-start = (bf16[4,12,3,512]{3,2,1,0:T(4,128)(2,1)S(1)}, bf16[4,12,3,512]{3,2,1,0:T(4,128)(2,1)S(1)}, u32[]{:S(2)}, u32[]{:S(2)}) collective-permute-start(bf16[4,12,3,512]{3,2,1,0:T(4,128)(2,1)S(1)} %get-tuple-element.17), channel_id=1, source_target_pairs={{0,32},{32,64},{64,96},{96,0},{1,33},{33,65},{65,97},{97,1},{2,34}... | collective-permute-start | bytes 442376 | tf_op jit(solution)/shard_map/ppermute | solution.py:31
  4.4 0.0 collective-permute-start.1
  4.4 3.7 %fusion.3 = (bf16[2,6,96,512]{3,2,1,0:T(8,128)(2,1)S(1)}, bf16[2,6,96,512]{3,2,1,0:T(8,128)(2,1)S(1)}, bf16[2,6,96,512]{3,2,1,0:T(8,128)(2,1)S(1)}, bf16[2,6,96,512]{3,2,1,0:T(8,128)(2,1)}) fusion(bf16[4,12,96,512]{3,2,1,0:T(8,128)(2,1)} %bitcast.11), kind=kLoop, calls=%fused_computation.11 | loop fusion | bytes 9437184 | tf_op jit(solution)/shard_map/slice | solution.py:293
  8.1 0.6 collective-permute-done
  8.8 0.7 collective-permute-done.1
  9.5 0.2 fusion.2.refs_5_
  9.7 0.8 fusion.5
  10.5 1.2 pad_maximum_fusion.2
  11.7 1.2 collective-permute-start.2
  12.9 0.0 copy-start.13
  12.9 0.0 copy-start.2
  12.9 1.2 pad_maximum_fusion.3
  14.1 6.9 %collective-permute-start.3 = (bf16[2,6,112,512]{3,2,1,0:T(8,128)(2,1)}, bf16[2,6,112,512]{3,2,1,0:T(8,128)(2,1)}, u32[]{:S(2)}, u32[]{:S(2)}) collective-permute-start(bf16[2,6,112,512]{3,2,1,0:T(8,128)(2,1)} %pad_maximum_fusion.3), channel_id=1, source_target_pairs={{0,31},{1,0},{2,1},{3,2},{4,3},{5,4},{6,5},{7,6},{8,7},{9,8},{10,9... | collective-permute-start | bytes 4128776 | tf_op jit(solution)/shard_map/ppermute | solution.py:31
  21.0 0.1 add_convert_fusion.refs_0_
  21.1 0.0 copy-done.13
  21.1 0.0 copy-start
  21.1 0.0 copy-start.1
  21.1 0.0 copy-start.3
  21.1 0.0 copy-start.4
  21.1 0.0 copy-start.5
  21.1 0.0 copy-start.6
  21.1 0.0 copy-start.7
  21.1 0.0 copy-start.8
  21.2 0.0 copy-start.9
  21.2 0.0 copy-start.10
  21.2 0.0 copy-start.11
  21.2 0.0 copy-start.12
  21.2 1.8 %pad_maximum_fusion = (bf16[2,6,112,512]{3,2,1,0:T(8,128)(2,1)S(1)}, bf16[2,6,112,512]{3,2,1,0:T(8,128)(2,1)S(1)}) fusion(bf16[2,6,16,512]{3,2,1,0:T(8,128)(2,1)} %get-tuple-element.22, bf16[2,6,96,512]{3,2,1,0:T(8,128)(2,1)} %get-tuple-element.16, bf16[2,6,16,512]{3,2,1,0:T(8,128)(2,1)} %get-tuple-element.21, bf16[2,6,96,512]{3,2,1,0:T(8,128)(2,1)S(1)} %get-tuple-element.15), kind=kLoop, calls=%fused_computation.4 | loop fusion | flops 5505024 | bytes 5505024 | tf_op jit(solution)/shard_map/concatenate | solution.py:293
  23.0 27.8 %collective-permute-done.2.refs_3_ = bf16[2,6,112,512]{3,2,1,0:T(8,128)(2,1)} collective-permute-done((bf16[2,6,112,512]{3,2,1,0:T(8,128)(2,1)}, bf16[2,6,112,512]{3,2,1,0:T(8,128)(2,1)}, u32[]{:S(2)}, u32[]{:S(2)}) %collective-permute-start.2) | collective-permute-done | bytes 1376288 | tf_op jit(solution)/shard_map/ppermute | solution.py:31
  50.8 0.2 collective-permute-done.3.refs_4_
  51.0 0.0 collective-permute-start.4
  51.0 7.9 %collective-permute-start.5 = (bf16[2,6,112,512]{3,2,1,0:T(8,128)(2,1)S(1)}, bf16[2,6,112,512]{3,2,1,0:T(8,128)(2,1)S(1)}, u32[]{:S(2)}, u32[]{:S(2)}) collective-permute-start(bf16[2,6,112,512]{3,2,1,0:T(8,128)(2,1)S(1)} %get-tuple-element.10), channel_id=1, source_target_pairs={{0,31},{1,0},{2,1},{3,2},{4,3},{5,4},{6,5},{7,6},{8,7},{9,8},{10,9... | collective-permute-start | bytes 4128776 | tf_op jit(solution)/shard_map/ppermute | solution.py:31
  58.9 0.0 copy-done.2
  58.9 0.0 copy-done
  58.9 0.0 copy-done.1
  58.9 0.0 copy-done.3
  59.0 0.0 copy-done.4
  59.0 0.0 copy-done.5
  59.0 0.0 copy-done.6
  59.0 0.0 copy-done.7
  59.0 0.0 copy-done.8
  59.0 0.0 copy-done.9
  59.0 0.0 copy-done.10
  59.0 0.0 copy-done.11
  59.0 0.0 copy-done.12
  59.0 47.7 %shard_map.145.refs_19_ = bf16[4,12,96,512]{3,2,1,0:T(8,128)(2,1)} custom-call(f32[2]{0:T(128)S(1)} %add_convert_fusion.refs_0_, f32[8]{0:T(128)S(1)} %broadcast_multiply_fusion.refs_1_, bf16[4,12,96,512]{3,2,1,0:T(8,128)(2,1)} %bitcast.12, bf16[2,6,112,512]{3,2,1,0:T(8,128)(2,1)} %collective-permute-done.2.refs_3_, ...), custom_call_target="tpu_custom_call" | custom-call | flops 24000000000 | bytes 20000000 | tf_op jit(solution)/shard_map/pallas_call | solution.py:238
  106.8 0.0 collective-permute-done.4.refs_3_
  106.8 0.0 collective-permute-done.5.refs_4_
  106.8 47.1 %shard_map.146 = bf16[4,12,96,512]{3,2,1,0:T(8,128)(2,1)} custom-call(f32[2]{0:T(128)S(1)} %add_convert_fusion.refs_0_, f32[8]{0:T(128)S(1)} %broadcast_multiply_fusion.refs_1_, bf16[4,12,96,512]{3,2,1,0:T(8,128)(2,1)} %bitcast.13, bf16[2,6,112,512]{3,2,1,0:T(8,128)(2,1)S(1)} %collective-permute-done.4.refs_3_, ...), custom_call_target="tpu_custom_call", output_to_operand_aliasing={{}: (19, {})} | custom-call | flops 24000000000 | bytes 20000000 | tf_op jit(solution)/shard_map/pallas_call | solution.py:238
  (1 shorter events, 0.0 us)
Async XLA Ops:
  1.3 7.5 %collective-permute-start = (bf16[4,12,3,512]{3,2,1,0:T(4,128)(2,1)S(1)}, bf16[4,12,3,512]{3,2,1,0:T(4,128)(2,1)S(1)}, u32[]{:S(2)}, u32[]{:S(2)}) collective-permute-start(bf16[4,12,3,512]{3,2,1,0:T(4,128)(2,1)S(1)} %get-tuple-element.17), channel_id=1, source_target_pairs={{0,32},{32,64},{64,96},{96,0},{1,33},{33,65},{65,97},{97,1},{2,34}... | collective-permute-start | bytes 442376 | tf_op jit(solution)/shard_map/ppermute | solution.py:31
  4.4 5.1 %collective-permute-start.1 = (bf16[4,12,3,512]{3,2,1,0:T(4,128)(2,1)S(1)}, bf16[4,12,3,512]{3,2,1,0:T(4,128)(2,1)S(1)}, u32[]{:S(2)}, u32[]{:S(2)}) collective-permute-start(bf16[4,12,3,512]{3,2,1,0:T(4,128)(2,1)S(1)} %get-tuple-element.18), channel_id=1, source_target_pairs={{0,96},{32,0},{64,32},{96,64},{1,97},{33,1},{65,33},{97,65},{2,98}... | collective-permute-start | bytes 442376 | tf_op jit(solution)/shard_map/ppermute | solution.py:31
  11.7 39.2 %collective-permute-start.2 = (bf16[2,6,112,512]{3,2,1,0:T(8,128)(2,1)}, bf16[2,6,112,512]{3,2,1,0:T(8,128)(2,1)}, u32[]{:S(2)}, u32[]{:S(2)}) collective-permute-start(bf16[2,6,112,512]{3,2,1,0:T(8,128)(2,1)} %pad_maximum_fusion.2), channel_id=1, source_target_pairs={{0,1},{1,2},{2,3},{3,4},{4,5},{5,6},{6,7},{7,8},{8,9},{9,10},{10,1... | collective-permute-start | bytes 4128776 | tf_op jit(solution)/shard_map/ppermute | solution.py:31
  12.9 8.2 %copy-start.13 = (f32[8]{0:T(128)S(1)}, f32[8]{0:T(128)}, u32[]{:S(2)}) copy-start(f32[8]{0:T(128)} %param.18) | copy-start | bytes 100
  12.9 46.1 %copy-start.2 = (bf16[512,1536]{1,0:T(8,128)(2,1)S(1)}, bf16[512,1536]{1,0:T(8,128)(2,1)}, u32[]{:S(2)}) copy-start(bf16[512,1536]{1,0:T(8,128)(2,1)} %refs_15_.3) | copy-start | bytes 4718596
  14.1 36.9 %collective-permute-start.3 = (bf16[2,6,112,512]{3,2,1,0:T(8,128)(2,1)}, bf16[2,6,112,512]{3,2,1,0:T(8,128)(2,1)}, u32[]{:S(2)}, u32[]{:S(2)}) collective-permute-start(bf16[2,6,112,512]{3,2,1,0:T(8,128)(2,1)} %pad_maximum_fusion.3), channel_id=1, source_target_pairs={{0,31},{1,0},{2,1},{3,2},{4,3},{5,4},{6,5},{7,6},{8,7},{9,8},{10,9... | collective-permute-start | bytes 4128776 | tf_op jit(solution)/shard_map/ppermute | solution.py:31
  21.1 37.9 %copy-start = (bf16[512,2048]{1,0:T(8,128)(2,1)S(1)}, bf16[512,2048]{1,0:T(8,128)(2,1)}, u32[]{:S(2)}) copy-start(bf16[512,2048]{1,0:T(8,128)(2,1)} %refs_17_.3) | copy-start | bytes 6291460
  21.1 37.9 %copy-start.1 = (bf16[2048,512]{1,0:T(8,128)(2,1)S(1)}, bf16[2048,512]{1,0:T(8,128)(2,1)}, u32[]{:S(2)}) copy-start(bf16[2048,512]{1,0:T(8,128)(2,1)} %refs_18_.3) | copy-start | bytes 6291460
  21.1 37.9 %copy-start.3 = (bf16[512,512]{1,0:T(8,128)(2,1)S(1)}, bf16[512,512]{1,0:T(8,128)(2,1)}, u32[]{:S(2)}) copy-start(bf16[512,512]{1,0:T(8,128)(2,1)} %refs_16_.3) | copy-start | bytes 1572868
  21.1 37.9 %copy-start.4 = (f32[512]{0:T(512)S(1)}, f32[512]{0:T(512)}, u32[]{:S(2)}) copy-start(f32[512]{0:T(512)} %param.16) | copy-start | bytes 6148
  21.1 37.9 %copy-start.5 = (f32[512]{0:T(512)S(1)}, f32[512]{0:T(512)}, u32[]{:S(2)}) copy-start(f32[512]{0:T(512)} %param.20) | copy-start | bytes 6148
  21.1 37.9 %copy-start.6 = (f32[144,144]{1,0:T(8,128)S(1)}, f32[144,144]{1,0:T(8,128)}, u32[]{:S(2)}) copy-start(f32[144,144]{1,0:T(8,128)} %constant.34.clone.refs_12_) | copy-start | bytes 248836
  21.1 37.9 %copy-start.7 = (bf16[192,256]{1,0:T(8,128)(2,1)S(1)}, bf16[192,256]{1,0:T(8,128)(2,1)}, u32[]{:S(2)}) copy-start(bf16[192,256]{1,0:T(8,128)(2,1)} %constant.29.clone.refs_7_) | copy-start | bytes 294916
  21.1 37.9 %copy-start.8 = (bf16[192,256]{1,0:T(8,128)(2,1)S(1)}, bf16[192,256]{1,0:T(8,128)(2,1)}, u32[]{:S(2)}) copy-start(bf16[192,256]{1,0:T(8,128)(2,1)} %constant.28.clone.refs_6_) | copy-start | bytes 294916
  21.2 37.9 %copy-start.9 = (bf16[128,144]{1,0:T(8,128)(2,1)S(1)}, bf16[128,144]{1,0:T(8,128)(2,1)}, u32[]{:S(2)}) copy-start(bf16[128,144]{1,0:T(8,128)(2,1)} %constant.33.clone.refs_11_) | copy-start | bytes 110596
  21.2 37.8 %copy-start.10 = (bf16[128,168]{1,0:T(8,128)(2,1)S(1)}, bf16[128,168]{1,0:T(8,128)(2,1)}, u32[]{:S(2)}) copy-start(bf16[128,168]{1,0:T(8,128)(2,1)} %constant.32.clone.refs_10_) | copy-start | bytes 129028
  21.2 37.8 %copy-start.11 = (bf16[128,144]{1,0:T(8,128)(2,1)S(1)}, bf16[128,144]{1,0:T(8,128)(2,1)}, u32[]{:S(2)}) copy-start(bf16[128,144]{1,0:T(8,128)(2,1)} %constant.31.clone.refs_9_) | copy-start | bytes 110596
  21.2 37.8 %copy-start.12 = (bf16[24,128]{1,0:T(8,128)(2,1)S(1)}, bf16[24,128]{1,0:T(8,128)(2,1)}, u32[]{:S(2)}) copy-start(bf16[24,128]{1,0:T(8,128)(2,1)} %constant.30.clone.refs_8_) | copy-start | bytes 18436
  51.0 55.8 %collective-permute-start.4 = (bf16[2,6,112,512]{3,2,1,0:T(8,128)(2,1)S(1)}, bf16[2,6,112,512]{3,2,1,0:T(8,128)(2,1)S(1)}, u32[]{:S(2)}, u32[]{:S(2)}) collective-permute-start(bf16[2,6,112,512]{3,2,1,0:T(8,128)(2,1)S(1)} %get-tuple-element.9), channel_id=1, source_target_pairs={{0,1},{1,2},{2,3},{3,4},{4,5},{5,6},{6,7},{7,8},{8,9},{9,10},{10,1... | collective-permute-start | bytes 4128776 | tf_op jit(solution)/shard_map/ppermute | solution.py:31
  51.0 55.8 %collective-permute-start.5 = (bf16[2,6,112,512]{3,2,1,0:T(8,128)(2,1)S(1)}, bf16[2,6,112,512]{3,2,1,0:T(8,128)(2,1)S(1)}, u32[]{:S(2)}, u32[]{:S(2)}) collective-permute-start(bf16[2,6,112,512]{3,2,1,0:T(8,128)(2,1)S(1)} %get-tuple-element.10), channel_id=1, source_target_pairs={{0,31},{1,0},{2,1},{3,2},{4,3},{5,4},{6,5},{7,6},{8,7},{9,8},{10,9... | collective-permute-start | bytes 4128776 | tf_op jit(solution)/shard_map/ppermute | solution.py:31

commit v4 on v3

--- a/solution.py
+++ b/solution.py
@@ -95,20 +95,101 @@
     return jnp.asarray(np.where(i[:, None] == i[None, :], 0.0, -1e30), jnp.float32)
 
 
+def gather(plan, pick_refs, main_ref, edge_of, first_col, side, dest):
+    for g in range(GROUPS):
+        slabs = [(s // HALF_LON, s % HALF_LON) for s in range(g * SLABS, (g + 1) * SLABS)]
+        at = (side * GROUPS + g) * PIECE
+        for table, (bands, segments) in zip(pick_refs, plan.picks):
+            stacked = jnp.concatenate(
+                [
+                    edge_of(level, col) if name == "edge" else main_ref[level, first_col + col, r0:r1, :]
+                    for name, r0, r1 in segments
+                    for level, col in slabs
+                ],
+                axis=0,
+            )
+            picked = jnp.dot(table[...], stacked, preferred_element_type=jnp.float32)
+            for n, band in enumerate(bands):
+                dest[band, at:at + PIECE, :] = picked[n * PIECE:(n + 1) * PIECE]
+
+
+def project_kernel(plan, *refs):
+    refs = list(refs)
+    own_ref, edge_ref = refs[:2]
+    pick_refs = refs[2:2 + len(plan.picks)]
+    gain_ref, weight_ref, xw_hbm, qkv_hbm, full_ref, xw_ref, qkv_ref, xsem, qsem = refs[2 + len(plan.picks):]
+    pair = pl.program_id(0)
+    for side in (0, 1):
+        first = side * HALF_LON
+        gather(plan, pick_refs, own_ref, lambda l, c: edge_ref[l, first + c], first, side, full_ref)
+    gain = gain_ref[...]
+
+    def copies(b):
+        return (
+            pltpu.make_async_copy(xw_ref.at[b], xw_hbm.at[pair, b], xsem.at[b]),
+            pltpu.make_async_copy(qkv_ref.at[b], qkv_hbm.at[pair, b], qsem.at[b]),
+        )
+
+    def step(b, carry):
+        values = full_ref[b]
+        xw_ref[b] = values.astype(jnp.bfloat16)
+        normed = norm_rows(values, gain).astype(jnp.bfloat16)
+        qkv_ref[b] = jnp.dot(normed, weight_ref[...], preferred_element_type=jnp.float32).astype(jnp.bfloat16)
+        for copy in copies(b):
+            copy.start()
+        return carry
+
+    lax.fori_loop(0, plan.count, step, 0)
+
+    def finish(b, carry):
+        for copy in copies(b):
+            copy.wait()
+        return carry
+
+    lax.fori_loop(0, plan.count, finish, 0)
+
+
+def project(plan, x, edges, gain, weight):
+    levels, cols, rows, channels = x.shape
+    pairs = levels // WL
+    whole = lambda a: pl.BlockSpec(a.shape, lambda i, n=a.ndim: (0,) * n)
+    mine = lambda r: pl.BlockSpec((WL, cols, r, channels), lambda i: (i, 0, 0, 0))
+    hbm = pl.BlockSpec(memory_space=pl.ANY)
+    small = [*plan.tables[:len(plan.picks)], gain, weight]
+    shape = lambda width: (plan.count, TOKENS, width)
+    return pl.pallas_call(
+        functools.partial(project_kernel, plan),
+        grid=(pairs,),
+        out_shape=[jax.ShapeDtypeStruct((pairs, *shape(n)), jnp.bfloat16) for n in (channels, weight.shape[1])],
+        in_specs=[mine(rows), mine(TILE)] + [whole(a) for a in small],
+        out_specs=[hbm, hbm],
+        scratch_shapes=[
+            pltpu.VMEM(shape(channels), jnp.float32),
+            pltpu.VMEM(shape(channels), jnp.bfloat16),
+            pltpu.VMEM(shape(weight.shape[1]), jnp.bfloat16),
+            pltpu.SemaphoreType.DMA((plan.count,)),
+            pltpu.SemaphoreType.DMA((plan.count,)),
+        ],
+        compiler_params=pltpu.CompilerParams(vmem_limit_bytes=VMEM_LIMIT),
+        cost_estimate=pl.CostEstimate(flops=8_000_000_000, bytes_accessed=26_000_000, transcendentals=0),
+    )(x, edges, *small)
+
+
 def block_kernel(plan, pair, aliased, *refs):
     refs = list(refs)
     pop = lambda: refs.pop(0)
     seam_ref, factor_ref = pop(), pop()
-    own_ref, around_refs, edge_ref = pop(), (pop(), pop()), pop()
+    around_refs = pop(), pop()
     pick_refs = [pop() for _ in plan.picks]
     place_refs = [pop() for _ in plan.places]
     bias_ref, gain_ref, gain2_ref = pop(), pop(), pop()
+    xw_hbm, mine_hbm = pop(), pop()
     weights_hbm = [pop() for _ in range(4)]
     if aliased:
         pop()
     out_ref = pop()
     weights = [pop() for _ in range(4)]
-    xw_ref, hw_ref, att_ref, yw_ref, ow_ref, wsem, osem = refs
+    xw_ref, mine_ref, hw_ref, att_ref, yw_ref, ow_ref, xsem, qsem, wsem, osem = refs
     qkv_ref, wo_ref, up_ref, down_ref = weights
     channels = xw_ref.shape[-1]
     heads = factor_ref.shape[0]
@@ -116,37 +197,30 @@
     group_heads = 256 // head_dim
     count = plan.count
 
+    def arriving(b):
+        return (
+            pltpu.make_async_copy(xw_hbm.at[pair, b], xw_ref.at[b], xsem.at[b]),
+            pltpu.make_async_copy(mine_hbm.at[pair, b], mine_ref.at[b], qsem.at[b]),
+        )
+
     copies = [pltpu.make_async_copy(a, b, wsem.at[i]) for i, (a, b) in enumerate(zip(weights_hbm, weights))]
-    for copy in copies:
-        copy.start()
-
-    for dest, side in ((xw_ref, 0), (xw_ref, 1), (hw_ref, 0), (hw_ref, 1)):
-        own = dest is xw_ref
-
-        def rows_of(name, s, r0, r1):
-            level, col = s // HALF_LON, s % HALF_LON + (side * HALF_LON if own else 0)
-            if name == "edge":
-                return edge_ref[level, col] if own else around_refs[side][level, col, plan.rows:plan.rows + TILE, :]
-            ref = own_ref if own else around_refs[side]
-            return ref[level, col, r0:r1, :]
-
-        for g in range(GROUPS):
-            ids = range(g * SLABS, (g + 1) * SLABS)
-            at = (side * GROUPS + g) * PIECE
-            for table, (bands, segments) in zip(pick_refs, plan.picks):
-                stacked = jnp.concatenate([rows_of(n, s, r0, r1) for n, r0, r1 in segments for s in ids], axis=0)
-                picked = jnp.dot(table[...], stacked, preferred_element_type=jnp.float32)
-                for n, band in enumerate(bands):
-                    dest[band, at:at + PIECE, :] = picked[n * PIECE:(n + 1) * PIECE]
+    copies[0].start()
+    for b in range(count):
+        for copy in arriving(b):
+            copy.start()
+        if b == 1:
+            for copy in copies[1:]:
+                copy.start()
+    for side, ref in enumerate(around_refs):
+        gather(plan, pick_refs, ref, lambda l, c: ref[l, c, plan.rows:plan.rows + TILE, :], 0, side, hw_ref)
 
     lane = lax.broadcasted_iota(jnp.int32, (1, 256), 1) // head_dim
     gain, gain2 = gain_ref[...], gain2_ref[...]
     copies[0].wait()
 
     def attend(b, bias):
-        normed = norm_rows(xw_ref[b], gain).astype(jnp.bfloat16)
         around = norm_rows(hw_ref[b], gain).astype(jnp.bfloat16)
-        mine = jnp.dot(normed, qkv_ref[...], preferred_element_type=jnp.float32)
+        mine = mine_ref[b].astype(jnp.float32)
         other = jnp.dot(around, qkv_ref[:, channels:], preferred_element_type=jnp.float32)
         for g in range(heads // group_heads):
             at = g * 256
@@ -182,7 +256,7 @@
             att_ref[b, :, at:at + 256] = jnp.concatenate(mixed, axis=0).astype(jnp.bfloat16)
 
     def feed(b):
-        residual = xw_ref[b] + jnp.dot(att_ref[b], wo_ref[...], preferred_element_type=jnp.float32)
+        residual = xw_ref[b].astype(jnp.float32) + jnp.dot(att_ref[b], wo_ref[...], preferred_element_type=jnp.float32)
         normed = norm_rows(residual, gain2).astype(jnp.bfloat16)
         acts = gelu(jnp.dot(normed, up_ref[...], preferred_element_type=jnp.float32)).astype(jnp.bfloat16)
         result = residual + jnp.dot(acts, down_ref[...], preferred_element_type=jnp.float32)
@@ -191,16 +265,22 @@
         for g in range(2 * GROUPS):
             yw_ref[g, pl.ds(at, PIECE), :] = result[g * PIECE:(g + 1) * PIECE]
 
+    for copy in arriving(0):
+        copy.wait()
     attend(0, bias_ref[...] * seam_ref[0])
     for copy in copies[1:]:
         copy.wait()
 
     def step(b, carry):
+        for copy in arriving(b):
+            copy.wait()
         feed(b - 1)
         attend(b, None)
         return carry
 
     lax.fori_loop(1, count - 1, step, 0)
+    for copy in arriving(count - 1):
+        copy.wait()
     feed(count - 2)
     attend(count - 1, bias_ref[...] * seam_ref[1])
     feed(count - 1)
@@ -219,17 +299,16 @@
     copy.wait()
 
 
-def block(plan, pair, seam, factor, x, around, edges, bias, gains, weights, out):
-    levels, cols, rows, channels = x.shape
+def block(plan, pair, seam, factor, shape, around, bias, gains, own, weights, out):
+    levels, cols, rows, channels = shape
     once = pl.Buffered(1)
     whole = lambda a: pl.BlockSpec(a.shape, lambda i, n=a.ndim: (0,) * n, pipeline_mode=once)
     smem = pl.BlockSpec(memory_space=pltpu.SMEM)
     hbm = pl.BlockSpec(memory_space=pl.ANY)
-    mine = lambda r: pl.BlockSpec((WL, cols, r, channels), lambda i: (pair, 0, 0, 0), pipeline_mode=once)
-    small = [*plan.tables, bias, *gains]
-    operands = [seam, factor, x, *around, edges, *small, *weights]
-    specs = [smem, smem, mine(rows), whole(around[0]), whole(around[1]), mine(TILE)]
-    specs += [whole(a) for a in small] + [hbm] * len(weights)
+    small = [*around, *plan.tables, bias, *gains]
+    large = [*own, *weights]
+    operands = [seam, factor, *small, *large]
+    specs = [smem, smem] + [whole(a) for a in small] + [hbm] * len(large)
     aliases = {}
     if out is not None:
         aliases = {len(operands): 0}
@@ -238,16 +317,19 @@
     return pl.pallas_call(
         functools.partial(block_kernel, plan, pair, out is not None),
         grid=(1,),
-        out_shape=jax.ShapeDtypeStruct(x.shape, jnp.bfloat16),
+        out_shape=jax.ShapeDtypeStruct(shape, jnp.bfloat16),
         in_specs=specs,
         out_specs=hbm,
         scratch_shapes=[pltpu.VMEM(w.shape, w.dtype) for w in weights]
         + [
-            pltpu.VMEM((plan.count, TOKENS, channels), jnp.float32),
+            pltpu.VMEM((plan.count, TOKENS, channels), jnp.bfloat16),
+            pltpu.VMEM((plan.count, TOKENS, own[1].shape[-1]), jnp.bfloat16),
             pltpu.VMEM((plan.count, TOKENS, channels), jnp.float32),
             pltpu.VMEM((plan.count, TOKENS, channels), jnp.bfloat16),
             pltpu.VMEM((2 * GROUPS, plan.count * PIECE, channels), jnp.float32),
             pltpu.VMEM((WL, cols, rows, channels), jnp.bfloat16),
+            pltpu.SemaphoreType.DMA((plan.count,)),
+            pltpu.SemaphoreType.DMA((plan.count,)),
             pltpu.SemaphoreType.DMA((len(weights),)),
             pltpu.SemaphoreType.DMA,
         ],
@@ -285,18 +367,23 @@
     gap = ((0, 0), (0, 0), (0, TILE // 2 - HALF_LAT), (0, 0))
     edges = jnp.concatenate([jnp.pad(above, gap), jnp.pad(below, gap)], axis=2)
 
-    out = None
-    around = []
-    for p in range(pairs):
+    def send(p, own):
         level = slice(WL * p, WL * p + WL)
         left, right = [
             jnp.concatenate([x[level, c], edges[level, c]], axis=2) for c in (slice(HALF_LON, cols), slice(0, HALF_LON))
         ]
-        if p > 0:
-            left, right, *around[-1] = lax.optimization_barrier((left, right, *around[-1]))
-        around.append([from_behind(left, "lon", 1), from_behind(right, "lon", -1)])
+        if own is not None:
+            left, right, *own = lax.optimization_barrier((left, right, *own))
+        return [from_behind(left, "lon", 1), from_behind(right, "lon", -1)], own
+
+    around, own = [None] * pairs, None
+    around[0], _ = send(0, None)
+    own = project(plan, x, edges, gains[0], triple_weight)
+    for p in range(1, pairs):
+        around[p], own = send(p, own)
+    out = None
     for p in range(pairs):
-        out = block(plan, p, seam, factor, x, around[p], edges, bias, gains, weights, out)
+        out = block(plan, p, seam, factor, x.shape, around[p], bias, gains, own, weights, out)
     return out.transpose(0, 2, 1, 3)
 
 

time: 154 us -> 142 us (0.922)
  waiting for transfers between devices: 29.4 us -> 0.79 us
  Pallas kernels: 94.9 us -> 108 us
  local copies, waits for them, and re-layouts: 5.94 us -> 8.96 us
    ppermute x6, waiting for transfers between devices: 29.4 us -> 0.79 us  [from_behind(): lax.ppermute(shard, axis, [(i, (i + by) % count) for i in range(count)])]
    pallas_call x0 -> x1, Pallas kernels: none -> 22.9 us  [project(): pl.pallas_call(functools.partial(project_kernel, plan), grid=(pairs,), ou...]
    pallas_call x2, Pallas kernels: 94.9 us -> 85.3 us  [block(): pl.pallas_call(functools.partial(block_kernel, plan, pair, out is not Non...]
    unnamed x28 -> x30, local copies, waits for them, and re-layouts: 0.08 us -> 2.54 us
  transfers between devices with their start and end apart: 6 -> 6, of which waited for: 4 -> 2; matrix products, arithmetic and copies ran while one was open for 4% -> 5% of each run, Pallas kernels for 31% -> 46%
where the time goes in v4:
time: 142 us
  Pallas kernels  108 us (76%)
  starting transfers between devices  18.5 us (13%)
  local copies, waits for them, and re-layouts  8.96 us (6%)
  other arithmetic  4.75 us (3%)
    pallas_call x2, Pallas kernels, block(): pl.pallas_call(functools.partial(block_kernel, plan, pair, out is not Non...  85.3 us
    pallas_call x1, Pallas kernels, project(): pl.pallas_call(functools.partial(project_kernel, plan), grid=(pairs,), ou...  22.9 us
    ppermute x6, starting transfers between devices, from_behind(): lax.ppermute(shard, axis, [(i, (i + by) % count) for i in range(count)])  18.5 us
    concatenate x3, other arithmetic, send(): jnp.concatenate([x[level, c], edges[level, c]], axis=2)  4.5 us
    slice x1, local copies, waits for them, and re-layouts, send(): x[level, c]  4.31 us
  transfers between devices with their start and end apart: 6, of which 2 were waited for; matrix products, arithmetic and copies ran while one was open for 5% of the time, Pallas kernels for 46%

profile of v4, /device:TPU:1, one launch (start us, length us, event | category | flops | bytes accessed | tf_op | source)
XLA Modules:
  0.0 141.7 jit_solution(4412229008013892082)
XLA Ops:
  0.0 1.3 fusion.4
  1.3 3.1 %collective-permute-start = (bf16[4,12,3,512]{3,2,1,0:T(4,128)(2,1)S(1)}, bf16[4,12,3,512]{3,2,1,0:T(4,128)(2,1)S(1)}, u32[]{:S(2)}, u32[]{:S(2)}) collective-permute-start(bf16[4,12,3,512]{3,2,1,0:T(4,128)(2,1)S(1)} %get-tuple-element.21), channel_id=1, source_target_pairs={{0,32},{32,64},{64,96},{96,0},{1,33},{33,65},{65,97},{97,1},{2,34}... | collective-permute-start | bytes 442376 | tf_op jit(solution)/shard_map/ppermute | solution.py:31
  4.4 0.0 collective-permute-start.1
  4.4 4.3 %fusion.3 = (bf16[2,6,96,512]{3,2,1,0:T(8,128)(2,1)S(1)}, bf16[2,6,96,512]{3,2,1,0:T(8,128)(2,1)S(1)}, bf16[2,6,96,512]{3,2,1,0:T(8,128)(2,1)}, bf16[2,6,96,512]{3,2,1,0:T(8,128)(2,1)}) fusion(bf16[4,12,96,512]{3,2,1,0:T(8,128)(2,1)} %bitcast.7), kind=kLoop, calls=%fused_computation.11 | loop fusion | bytes 9437184 | tf_op jit(solution)/shard_map/slice | solution.py:373
  8.7 0.1 collective-permute-done
  8.8 0.7 collective-permute-done.1
  9.5 0.2 fusion.2.refs_1_
  9.6 0.8 fusion.5
  10.5 1.2 pad_maximum_fusion.2
  11.7 1.2 collective-permute-start.4
  12.9 0.0 copy-start.14
  12.9 1.2 pad_maximum_fusion.3
  14.1 6.9 %collective-permute-start.5 = (bf16[2,6,112,512]{3,2,1,0:T(8,128)(2,1)}, bf16[2,6,112,512]{3,2,1,0:T(8,128)(2,1)S(1)}, u32[]{:S(2)}, u32[]{:S(2)}) collective-permute-start(bf16[2,6,112,512]{3,2,1,0:T(8,128)(2,1)} %pad_maximum_fusion.3), channel_id=1, source_target_pairs={{0,31},{1,0},{2,1},{3,2},{4,3},{5,4},{6,5},{7,6},{8,7},{9,8},{10,9... | collective-permute-start | bytes 4128776 | tf_op jit(solution)/shard_map/ppermute | solution.py:31
  21.0 0.1 add_convert_fusion.refs_0_
  21.1 0.0 copy-done.14
  21.1 0.0 copy-start.3
  21.1 0.0 copy-start.5
  21.1 0.0 copy-start.8
  21.1 0.0 copy-start.9
  21.2 0.0 copy-start.13
  21.2 2.1 %pad_maximum_fusion = (bf16[2,6,112,512]{3,2,1,0:T(8,128)(2,1)S(1)}, bf16[2,6,112,512]{3,2,1,0:T(8,128)(2,1)S(1)}) fusion(bf16[2,6,16,512]{3,2,1,0:T(8,128)(2,1)} %get-tuple-element.26, bf16[2,6,96,512]{3,2,1,0:T(8,128)(2,1)} %get-tuple-element.20, bf16[2,6,16,512]{3,2,1,0:T(8,128)(2,1)} %get-tuple-element.25, bf16[2,6,96,512]{3,2,1,0:T(8,128)(2,1)} %get-tuple-element.19), kind=kLoop, calls=%fused_computation.4 | loop fusion | flops 5505024 | bytes 5505024 | tf_op jit(solution)/shard_map/concatenate | solution.py:373
  23.3 0.1 copy-done.3
  23.4 0.0 copy-done.5
  23.4 0.0 copy-done.8
  23.4 0.0 copy-done.9
  23.4 0.0 copy-done.13
  23.4 0.0 copy-start
  23.4 2.3 %copy-done = bf16[4,96,12,512]{3,1,2,0:T(8,128)(2,1)S(1)} copy-done((bf16[4,96,12,512]{3,1,2,0:T(8,128)(2,1)S(1)}, bf16[4,96,12,512]{3,1,2,0:T(8,128)(2,1)}, u32[]{:S(2)}) %copy-start) | copy-done | bytes 4718616
  25.7 0.0 copy-start.1
  25.7 0.0 copy-start.2
  25.8 0.0 copy-start.4
  25.8 0.0 copy-start.6
  25.8 0.0 copy-start.7
  25.8 0.0 copy-start.10
  25.8 0.0 copy-start.11
  25.8 0.0 copy-start.12
  25.8 22.9 %shard_map.145 = (bf16[2,17,144,512]{3,2,1,0:T(8,128)(2,1)}, bf16[2,17,144,1536]{3,2,1,0:T(8,128)(2,1)}) custom-call(bf16[4,12,96,512]{3,2,1,0:T(8,128)(2,1)S(1)} %bitcast.8, bf16[4,12,16,512]{3,2,1,0:T(8,128)(2,1)S(1)} %fusion.2.refs_1_, bf16[192,256]{1,0:T(8,128)(2,1)S(1)} %copy-done.9, bf16[192,256]{1,0:T(8,128)(2,1)S(1)} %copy-done.8, ...), custom_call_target="tpu_custom_call" | custom-call | flops 8000000000 | bytes 26000000 | tf_op jit(solution)/shard_map/pallas_call | solution.py:160
  48.7 0.1 collective-permute-start.2
  48.8 7.2 %collective-permute-start.3 = (bf16[2,6,112,512]{3,2,1,0:T(8,128)(2,1)S(1)}, bf16[2,6,112,512]{3,2,1,0:T(8,128)(2,1)S(1)}, u32[]{:S(2)}, u32[]{:S(2)}) collective-permute-start(bf16[2,6,112,512]{3,2,1,0:T(8,128)(2,1)S(1)} %get-tuple-element.14), channel_id=1, source_target_pairs={{0,31},{1,0},{2,1},{3,2},{4,3},{5,4},{6,5},{7,6},{8,7},{9,8},{10,9... | collective-permute-start | bytes 4128776 | tf_op jit(solution)/shard_map/ppermute | solution.py:31
  56.0 0.0 collective-permute-done.4.refs_2_
  56.0 0.0 collective-permute-done.5.refs_3_
  56.0 0.0 copy-done.1
  56.0 0.0 copy-done.2
  56.0 0.0 copy-done.4
  56.1 0.0 copy-done.6
  56.1 0.0 copy-done.7
  56.1 0.0 copy-done.10
  56.1 0.0 copy-done.11
  56.1 0.0 copy-done.12
  56.1 42.6 %shard_map.146.refs_19_ = bf16[4,12,96,512]{3,2,1,0:T(8,128)(2,1)} custom-call(f32[2]{0:T(128)S(1)} %add_convert_fusion.refs_0_, f32[8]{0:T(128)S(1)} %broadcast_multiply_fusion.refs_1_, bf16[2,6,112,512]{3,2,1,0:T(8,128)(2,1)S(1)} %collective-permute-done.4.refs_2_, bf16[2,6,112,512]{3,2,1,0:T(8,128)(2,1)S(1)} %collective-permute-done.5.refs_3_, ...), custom_call_target="tpu_custom_call" | custom-call | flops 24000000000 | bytes 20000000 | tf_op jit(solution)/shard_map/pallas_call | solution.py:317
  98.7 0.0 collective-permute-done.2.refs_2_
  98.7 0.0 collective-permute-done.3.refs_3_
  98.7 42.8 %shard_map.147 = bf16[4,12,96,512]{3,2,1,0:T(8,128)(2,1)} custom-call(f32[2]{0:T(128)S(1)} %add_convert_fusion.refs_0_, f32[8]{0:T(128)S(1)} %broadcast_multiply_fusion.refs_1_, bf16[2,6,112,512]{3,2,1,0:T(8,128)(2,1)S(1)} %collective-permute-done.2.refs_2_, ...), custom_call_target="tpu_custom_call", output_to_operand_aliasing={{}: (19, {})} | custom-call | flops 24000000000 | bytes 20000000 | tf_op jit(solution)/shard_map/pallas_call | solution.py:317
  (1 shorter events, 0.0 us)
Async XLA Ops:
  1.3 7.5 %collective-permute-start = (bf16[4,12,3,512]{3,2,1,0:T(4,128)(2,1)S(1)}, bf16[4,12,3,512]{3,2,1,0:T(4,128)(2,1)S(1)}, u32[]{:S(2)}, u32[]{:S(2)}) collective-permute-start(bf16[4,12,3,512]{3,2,1,0:T(4,128)(2,1)S(1)} %get-tuple-element.21), channel_id=1, source_target_pairs={{0,32},{32,64},{64,96},{96,0},{1,33},{33,65},{65,97},{97,1},{2,34}... | collective-permute-start | bytes 442376 | tf_op jit(solution)/shard_map/ppermute | solution.py:31
  4.4 5.1 %collective-permute-start.1 = (bf16[4,12,3,512]{3,2,1,0:T(4,128)(2,1)S(1)}, bf16[4,12,3,512]{3,2,1,0:T(4,128)(2,1)S(1)}, u32[]{:S(2)}, u32[]{:S(2)}) collective-permute-start(bf16[4,12,3,512]{3,2,1,0:T(4,128)(2,1)S(1)} %get-tuple-element.22), channel_id=1, source_target_pairs={{0,96},{32,0},{64,32},{96,64},{1,97},{33,1},{65,33},{97,65},{2,98}... | collective-permute-start | bytes 442376 | tf_op jit(solution)/shard_map/ppermute | solution.py:31
  11.7 44.3 %collective-permute-start.4 = (bf16[2,6,112,512]{3,2,1,0:T(8,128)(2,1)}, bf16[2,6,112,512]{3,2,1,0:T(8,128)(2,1)S(1)}, u32[]{:S(2)}, u32[]{:S(2)}) collective-permute-start(bf16[2,6,112,512]{3,2,1,0:T(8,128)(2,1)} %pad_maximum_fusion.2), channel_id=1, source_target_pairs={{0,1},{1,2},{2,3},{3,4},{4,5},{5,6},{6,7},{7,8},{8,9},{9,10},{10,1... | collective-permute-start | bytes 4128776 | tf_op jit(solution)/shard_map/ppermute | solution.py:31
  12.9 8.2 %copy-start.14 = (f32[8]{0:T(128)S(1)}, f32[8]{0:T(128)}, u32[]{:S(2)}) copy-start(f32[8]{0:T(128)} %param.18) | copy-start | bytes 100
  14.1 41.9 %collective-permute-start.5 = (bf16[2,6,112,512]{3,2,1,0:T(8,128)(2,1)}, bf16[2,6,112,512]{3,2,1,0:T(8,128)(2,1)S(1)}, u32[]{:S(2)}, u32[]{:S(2)}) collective-permute-start(bf16[2,6,112,512]{3,2,1,0:T(8,128)(2,1)} %pad_maximum_fusion.3), channel_id=1, source_target_pairs={{0,31},{1,0},{2,1},{3,2},{4,3},{5,4},{6,5},{7,6},{8,7},{9,8},{10,9... | collective-permute-start | bytes 4128776 | tf_op jit(solution)/shard_map/ppermute | solution.py:31
  21.1 2.3 %copy-start.3 = (bf16[512,1536]{1,0:T(8,128)(2,1)S(1)}, bf16[512,1536]{1,0:T(8,128)(2,1)}, u32[]{:S(2)}) copy-start(bf16[512,1536]{1,0:T(8,128)(2,1)} %refs_15_.3) | copy-start | bytes 4718596
  21.1 2.3 %copy-start.5 = (f32[512]{0:T(512)S(1)}, f32[512]{0:T(512)}, u32[]{:S(2)}) copy-start(f32[512]{0:T(512)} %param.16) | copy-start | bytes 6148
  21.1 2.3 %copy-start.8 = (bf16[192,256]{1,0:T(8,128)(2,1)S(1)}, bf16[192,256]{1,0:T(8,128)(2,1)}, u32[]{:S(2)}) copy-start(bf16[192,256]{1,0:T(8,128)(2,1)} %constant.29.clone.refs_3_.refs_5_) | copy-start | bytes 294916
  21.1 2.3 %copy-start.9 = (bf16[192,256]{1,0:T(8,128)(2,1)S(1)}, bf16[192,256]{1,0:T(8,128)(2,1)}, u32[]{:S(2)}) copy-start(bf16[192,256]{1,0:T(8,128)(2,1)} %constant.28.clone.refs_2_.refs_4_) | copy-start | bytes 294916
  21.2 2.2 %copy-start.13 = (bf16[24,128]{1,0:T(8,128)(2,1)S(1)}, bf16[24,128]{1,0:T(8,128)(2,1)}, u32[]{:S(2)}) copy-start(bf16[24,128]{1,0:T(8,128)(2,1)} %constant.30.clone.refs_4_.refs_6_) | copy-start | bytes 18436
  23.4 2.3 %copy-start = (bf16[4,96,12,512]{3,1,2,0:T(8,128)(2,1)S(1)}, bf16[4,96,12,512]{3,1,2,0:T(8,128)(2,1)}, u32[]{:S(2)}) copy-start(bf16[4,96,12,512]{3,1,2,0:T(8,128)(2,1)} %param.15) | copy-start | bytes 14155780
  25.7 30.3 %copy-start.1 = (bf16[512,2048]{1,0:T(8,128)(2,1)S(1)}, bf16[512,2048]{1,0:T(8,128)(2,1)}, u32[]{:S(2)}) copy-start(bf16[512,2048]{1,0:T(8,128)(2,1)} %refs_17_.3) | copy-start | bytes 6291460
  25.7 30.3 %copy-start.2 = (bf16[2048,512]{1,0:T(8,128)(2,1)S(1)}, bf16[2048,512]{1,0:T(8,128)(2,1)}, u32[]{:S(2)}) copy-start(bf16[2048,512]{1,0:T(8,128)(2,1)} %refs_18_.3) | copy-start | bytes 6291460
  25.8 30.3 %copy-start.4 = (bf16[512,512]{1,0:T(8,128)(2,1)S(1)}, bf16[512,512]{1,0:T(8,128)(2,1)}, u32[]{:S(2)}) copy-start(bf16[512,512]{1,0:T(8,128)(2,1)} %refs_16_.3) | copy-start | bytes 1572868
  25.8 30.3 %copy-start.6 = (f32[512]{0:T(512)S(1)}, f32[512]{0:T(512)}, u32[]{:S(2)}) copy-start(f32[512]{0:T(512)} %param.20) | copy-start | bytes 6148
  25.8 30.3 %copy-start.7 = (f32[144,144]{1,0:T(8,128)S(1)}, f32[144,144]{1,0:T(8,128)}, u32[]{:S(2)}) copy-start(f32[144,144]{1,0:T(8,128)} %constant.34.clone.refs_10_) | copy-start | bytes 248836
  25.8 30.3 %copy-start.10 = (bf16[128,144]{1,0:T(8,128)(2,1)S(1)}, bf16[128,144]{1,0:T(8,128)(2,1)}, u32[]{:S(2)}) copy-start(bf16[128,144]{1,0:T(8,128)(2,1)} %constant.33.clone.refs_9_) | copy-start | bytes 110596
  25.8 30.3 %copy-start.11 = (bf16[128,168]{1,0:T(8,128)(2,1)S(1)}, bf16[128,168]{1,0:T(8,128)(2,1)}, u32[]{:S(2)}) copy-start(bf16[128,168]{1,0:T(8,128)(2,1)} %constant.32.clone.refs_8_) | copy-start | bytes 129028
  25.8 30.3 %copy-start.12 = (bf16[128,144]{1,0:T(8,128)(2,1)S(1)}, bf16[128,144]{1,0:T(8,128)(2,1)}, u32[]{:S(2)}) copy-start(bf16[128,144]{1,0:T(8,128)(2,1)} %constant.31.clone.refs_7_) | copy-start | bytes 110596
  48.7 49.9 %collective-permute-start.2 = (bf16[2,6,112,512]{3,2,1,0:T(8,128)(2,1)S(1)}, bf16[2,6,112,512]{3,2,1,0:T(8,128)(2,1)S(1)}, u32[]{:S(2)}, u32[]{:S(2)}) collective-permute-start(bf16[2,6,112,512]{3,2,1,0:T(8,128)(2,1)S(1)} %get-tuple-element.13), channel_id=1, source_target_pairs={{0,1},{1,2},{2,3},{3,4},{4,5},{5,6},{6,7},{7,8},{8,9},{9,10},{10,1... | collective-permute-start | bytes 4128776 | tf_op jit(solution)/shard_map/ppermute | solution.py:31
  48.8 49.9 %collective-permute-start.3 = (bf16[2,6,112,512]{3,2,1,0:T(8,128)(2,1)S(1)}, bf16[2,6,112,512]{3,2,1,0:T(8,128)(2,1)S(1)}, u32[]{:S(2)}, u32[]{:S(2)}) collective-permute-start(bf16[2,6,112,512]{3,2,1,0:T(8,128)(2,1)S(1)} %get-tuple-element.14), channel_id=1, source_target_pairs={{0,31},{1,0},{2,1},{3,2},{4,3},{5,4},{6,5},{7,6},{8,7},{9,8},{10,9... | collective-permute-start | bytes 4128776 | tf_op jit(solution)/shard_map/ppermute | solution.py:31

commit v5 on v4

--- a/solution.py
+++ b/solution.py
@@ -368,17 +368,18 @@
     edges = jnp.concatenate([jnp.pad(above, gap), jnp.pad(below, gap)], axis=2)
 
     def send(p, own):
+        source = (x, edges)
+        if own is not None:
+            *source, own[0], own[1] = lax.optimization_barrier((x, edges, *own))
         level = slice(WL * p, WL * p + WL)
         left, right = [
-            jnp.concatenate([x[level, c], edges[level, c]], axis=2) for c in (slice(HALF_LON, cols), slice(0, HALF_LON))
+            jnp.concatenate([a[level, c] for a in source], axis=2) for c in (slice(HALF_LON, cols), slice(0, HALF_LON))
         ]
-        if own is not None:
-            left, right, *own = lax.optimization_barrier((left, right, *own))
         return [from_behind(left, "lon", 1), from_behind(right, "lon", -1)], own
 
     around, own = [None] * pairs, None
     around[0], _ = send(0, None)
-    own = project(plan, x, edges, gains[0], triple_weight)
+    own = list(project(plan, x, edges, gains[0], triple_weight))
     for p in range(1, pairs):
         around[p], own = send(p, own)
     out = None

time: 142 us -> 136 us (0.958)
  local copies, waits for them, and re-layouts: 8.96 us -> 3.44 us
  other arithmetic: 4.75 us -> 1.73 us
  waiting for transfers between devices: 0.79 us -> 3.2 us
    slice x2 -> x4, local copies, waits for them, and re-layouts: 5.15 us -> 2.08 us  [send(): a[level, c]]
    concatenate x3 -> x4, other arithmetic: 4.5 us -> 1.47 us  [send(): jnp.concatenate([a[level, c] for a in source], axis=2)]
    unnamed x30, local copies, waits for them, and re-layouts: 2.54 us -> 0.08 us
    ppermute x6, waiting for transfers between devices: 0.79 us -> 3.2 us  [from_behind(): lax.ppermute(shard, axis, [(i, (i + by) % count) for i in range(count)])]
  transfers between devices with their start and end apart: 6 -> 6, of which waited for: 2 -> 2; matrix products, arithmetic and copies ran while one was open for 5% -> 2% of each run, Pallas kernels for 46% -> 48%
where the time goes in v5:
time: 136 us
  Pallas kernels  108 us (79%)
  starting transfers between devices  18.8 us (14%)
  local copies, waits for them, and re-layouts  3.44 us (3%)
  waiting for transfers between devices  3.2 us (2%)
  other arithmetic  1.73 us (1%)
    pallas_call x2, Pallas kernels, block(): pl.pallas_call(functools.partial(block_kernel, plan, pair, out is not Non...  85.1 us
    pallas_call x1, Pallas kernels, project(): pl.pallas_call(functools.partial(project_kernel, plan), grid=(pairs,), ou...  22.9 us
    ppermute x6, starting transfers between devices, from_behind(): lax.ppermute(shard, axis, [(i, (i + by) % count) for i in range(count)])  18.8 us
    ppermute x6, waiting for transfers between devices, from_behind(): lax.ppermute(shard, axis, [(i, (i + by) % count) for i in range(count)])  3.2 us
  transfers between devices with their start and end apart: 6, of which 2 were waited for; matrix products, arithmetic and copies ran while one was open for 2% of the time, Pallas kernels for 48%

profile of v5, /device:TPU:1, one launch (start us, length us, event | category | flops | bytes accessed | tf_op | source)
XLA Modules:
  0.0 135.7 jit_solution(12858582205069079472)
XLA Ops:
  0.0 1.3 fusion.5
  1.3 3.1 %collective-permute-start = (bf16[4,12,3,512]{3,2,1,0:T(4,128)(2,1)S(1)}, bf16[4,12,3,512]{3,2,1,0:T(4,128)(2,1)S(1)}, u32[]{:S(2)}, u32[]{:S(2)}) collective-permute-start(bf16[4,12,3,512]{3,2,1,0:T(4,128)(2,1)S(1)} %get-tuple-element.21), channel_id=1, source_target_pairs={{0,32},{32,64},{64,96},{96,0},{1,33},{33,65},{65,97},{97,1},{2,34}... | collective-permute-start | bytes 442376 | tf_op jit(solution)/shard_map/ppermute | solution.py:31
  4.4 0.0 copy-start.14
  4.4 0.0 collective-permute-start.1
  4.4 1.8 %fusion.3 = (bf16[2,6,96,512]{3,2,1,0:T(8,128)(2,1)S(1)}, bf16[2,6,96,512]{3,2,1,0:T(8,128)(2,1)S(1)}) fusion(bf16[4,12,96,512]{3,2,1,0:T(8,128)(2,1)} %bitcast.7), kind=kLoop, calls=%fused_computation.11 | loop fusion | bytes 4718592 | tf_op jit(solution)/shard_map/slice | solution.py:376
  6.2 0.0 copy-done.14
  6.2 0.1 add_convert_fusion.refs_0_
  6.3 2.5 %collective-permute-done = bf16[4,12,3,512]{3,2,1,0:T(4,128)(2,1)S(1)} collective-permute-done((bf16[4,12,3,512]{3,2,1,0:T(4,128)(2,1)S(1)}, bf16[4,12,3,512]{3,2,1,0:T(4,128)(2,1)S(1)}, u32[]{:S(2)}, u32[]{:S(2)}) %collective-permute-start) | collective-permute-done | bytes 147488 | tf_op jit(solution)/shard_map/ppermute | solution.py:31
  8.8 0.7 collective-permute-done.1
  9.5 0.0 copy-start.8
  9.5 0.0 copy-start.9
  9.5 0.2 fusion.2.refs_1_
  9.7 0.0 copy-start.3
  9.7 0.0 copy-start
  9.7 1.2 pad_maximum_fusion.2
  10.9 1.2 collective-permute-start.4
  12.1 0.0 copy-start.5
  12.1 0.0 copy-start.13
  12.1 0.1 pad_maximum_fusion.3
  12.2 7.0 %collective-permute-start.5 = (bf16[2,6,112,512]{3,2,1,0:T(8,128)(2,1)S(1)}, bf16[2,6,112,512]{3,2,1,0:T(8,128)(2,1)S(1)}, u32[]{:S(2)}, u32[]{:S(2)}) collective-permute-start(bf16[2,6,112,512]{3,2,1,0:T(8,128)(2,1)S(1)} %pad_maximum_fusion.3), channel_id=1, source_target_pairs={{0,31},{1,0},{2,1},{3,2},{4,3},{5,4},{6,5},{7,6},{8,7},{9,8},{10,9... | collective-permute-start | bytes 4128776 | tf_op jit(solution)/shard_map/ppermute | solution.py:31
  19.2 0.0 copy-done.8
  19.2 0.0 copy-done.9
  19.2 0.0 copy-done.3
  19.2 0.0 copy-done
  19.2 0.0 copy-done.5
  19.2 0.0 copy-done.13
  19.3 22.9 %shard_map.145 = (bf16[2,17,144,512]{3,2,1,0:T(8,128)(2,1)}, bf16[2,17,144,1536]{3,2,1,0:T(8,128)(2,1)}) custom-call(bf16[4,12,96,512]{3,2,1,0:T(8,128)(2,1)S(1)} %bitcast.8, bf16[4,12,16,512]{3,2,1,0:T(8,128)(2,1)S(1)} %fusion.2.refs_1_, bf16[192,256]{1,0:T(8,128)(2,1)S(1)} %copy-done.9, bf16[192,256]{1,0:T(8,128)(2,1)S(1)} %copy-done.8, ...), custom_call_target="tpu_custom_call" | custom-call | flops 8000000000 | bytes 26000000 | tf_op jit(solution)/shard_map/pallas_call | solution.py:160
  42.2 0.2 fusion.4
  42.5 0.0 copy-start.2
  42.5 0.0 copy-start.7
  42.5 0.0 copy-start.11
  42.5 0.0 copy-start.12
  42.5 0.1 pad_maximum_fusion
  42.6 0.1 collective-permute-start.2
  42.7 0.0 copy-start.1
  42.7 0.0 copy-start.4
  42.7 0.0 copy-start.6
  42.7 0.0 copy-start.10
  42.7 0.1 pad_maximum_fusion.1
  42.8 7.4 %collective-permute-start.3 = (bf16[2,6,112,512]{3,2,1,0:T(8,128)(2,1)S(1)}, bf16[2,6,112,512]{3,2,1,0:T(8,128)(2,1)S(1)}, u32[]{:S(2)}, u32[]{:S(2)}) collective-permute-start(bf16[2,6,112,512]{3,2,1,0:T(8,128)(2,1)S(1)} %pad_maximum_fusion.1), channel_id=1, source_target_pairs={{0,31},{1,0},{2,1},{3,2},{4,3},{5,4},{6,5},{7,6},{8,7},{9,8},{10,9... | collective-permute-start | bytes 4128776 | tf_op jit(solution)/shard_map/ppermute | solution.py:31
  50.3 0.0 collective-permute-done.4.refs_2_
  50.3 0.0 collective-permute-done.5.refs_3_
  50.3 0.0 copy-done.2
  50.3 0.0 copy-done.7
  50.3 0.0 copy-done.11
  50.3 0.0 copy-done.12
  50.3 0.0 copy-done.1
  50.3 0.0 copy-done.4
  50.3 0.0 copy-done.6
  50.3 0.0 copy-done.10
  50.3 42.4 %shard_map.146.refs_19_ = bf16[4,12,96,512]{3,2,1,0:T(8,128)(2,1)} custom-call(f32[2]{0:T(128)S(1)} %add_convert_fusion.refs_0_, f32[8]{0:T(128)S(1)} %broadcast_multiply_fusion.refs_1_, bf16[2,6,112,512]{3,2,1,0:T(8,128)(2,1)S(1)} %collective-permute-done.4.refs_2_, bf16[2,6,112,512]{3,2,1,0:T(8,128)(2,1)S(1)} %collective-permute-done.5.refs_3_, ...), custom_call_target="tpu_custom_call" | custom-call | flops 24000000000 | bytes 20000000 | tf_op jit(solution)/shard_map/pallas_call | solution.py:317
  92.8 0.0 collective-permute-done.2.refs_2_
  92.8 0.0 collective-permute-done.3.refs_3_
  92.8 42.7 %shard_map.147 = bf16[4,12,96,512]{3,2,1,0:T(8,128)(2,1)} custom-call(f32[2]{0:T(128)S(1)} %add_convert_fusion.refs_0_, f32[8]{0:T(128)S(1)} %broadcast_multiply_fusion.refs_1_, bf16[2,6,112,512]{3,2,1,0:T(8,128)(2,1)S(1)} %collective-permute-done.2.refs_2_, ...), custom_call_target="tpu_custom_call", output_to_operand_aliasing={{}: (19, {})} | custom-call | flops 24000000000 | bytes 20000000 | tf_op jit(solution)/shard_map/pallas_call | solution.py:317
  (3 shorter events, 0.1 us)
Async XLA Ops:
  1.3 7.5 %collective-permute-start = (bf16[4,12,3,512]{3,2,1,0:T(4,128)(2,1)S(1)}, bf16[4,12,3,512]{3,2,1,0:T(4,128)(2,1)S(1)}, u32[]{:S(2)}, u32[]{:S(2)}) collective-permute-start(bf16[4,12,3,512]{3,2,1,0:T(4,128)(2,1)S(1)} %get-tuple-element.21), channel_id=1, source_target_pairs={{0,32},{32,64},{64,96},{96,0},{1,33},{33,65},{65,97},{97,1},{2,34}... | collective-permute-start | bytes 442376 | tf_op jit(solution)/shard_map/ppermute | solution.py:31
  4.4 1.8 %copy-start.14 = (f32[8]{0:T(128)S(1)}, f32[8]{0:T(128)}, u32[]{:S(2)}) copy-start(f32[8]{0:T(128)} %param.18) | copy-start | bytes 100
  4.4 5.1 %collective-permute-start.1 = (bf16[4,12,3,512]{3,2,1,0:T(4,128)(2,1)S(1)}, bf16[4,12,3,512]{3,2,1,0:T(4,128)(2,1)S(1)}, u32[]{:S(2)}, u32[]{:S(2)}) collective-permute-start(bf16[4,12,3,512]{3,2,1,0:T(4,128)(2,1)S(1)} %get-tuple-element.22), channel_id=1, source_target_pairs={{0,96},{32,0},{64,32},{96,64},{1,97},{33,1},{65,33},{97,65},{2,98}... | collective-permute-start | bytes 442376 | tf_op jit(solution)/shard_map/ppermute | solution.py:31
  9.5 9.8 %copy-start.8 = (bf16[192,256]{1,0:T(8,128)(2,1)S(1)}, bf16[192,256]{1,0:T(8,128)(2,1)}, u32[]{:S(2)}) copy-start(bf16[192,256]{1,0:T(8,128)(2,1)} %constant.29.clone.refs_3_.refs_5_) | copy-start | bytes 294916
  9.5 9.8 %copy-start.9 = (bf16[192,256]{1,0:T(8,128)(2,1)S(1)}, bf16[192,256]{1,0:T(8,128)(2,1)}, u32[]{:S(2)}) copy-start(bf16[192,256]{1,0:T(8,128)(2,1)} %constant.28.clone.refs_2_.refs_4_) | copy-start | bytes 294916
  9.7 9.6 %copy-start.3 = (bf16[512,1536]{1,0:T(8,128)(2,1)S(1)}, bf16[512,1536]{1,0:T(8,128)(2,1)}, u32[]{:S(2)}) copy-start(bf16[512,1536]{1,0:T(8,128)(2,1)} %refs_15_.3) | copy-start | bytes 4718596
  9.7 9.5 %copy-start = (bf16[4,96,12,512]{3,1,2,0:T(8,128)(2,1)S(1)}, bf16[4,96,12,512]{3,1,2,0:T(8,128)(2,1)}, u32[]{:S(2)}) copy-start(bf16[4,96,12,512]{3,1,2,0:T(8,128)(2,1)} %param.15) | copy-start | bytes 14155780
  10.9 39.4 %collective-permute-start.4 = (bf16[2,6,112,512]{3,2,1,0:T(8,128)(2,1)}, bf16[2,6,112,512]{3,2,1,0:T(8,128)(2,1)S(1)}, u32[]{:S(2)}, u32[]{:S(2)}) collective-permute-start(bf16[2,6,112,512]{3,2,1,0:T(8,128)(2,1)} %pad_maximum_fusion.2), channel_id=1, source_target_pairs={{0,1},{1,2},{2,3},{3,4},{4,5},{5,6},{6,7},{7,8},{8,9},{9,10},{10,1... | collective-permute-start | bytes 4128776 | tf_op jit(solution)/shard_map/ppermute | solution.py:31
  12.1 7.1 %copy-start.5 = (f32[512]{0:T(512)S(1)}, f32[512]{0:T(512)}, u32[]{:S(2)}) copy-start(f32[512]{0:T(512)} %param.16) | copy-start | bytes 6148
  12.1 7.1 %copy-start.13 = (bf16[24,128]{1,0:T(8,128)(2,1)S(1)}, bf16[24,128]{1,0:T(8,128)(2,1)}, u32[]{:S(2)}) copy-start(bf16[24,128]{1,0:T(8,128)(2,1)} %constant.30.clone.refs_4_.refs_6_) | copy-start | bytes 18436
  12.2 38.0 %collective-permute-start.5 = (bf16[2,6,112,512]{3,2,1,0:T(8,128)(2,1)S(1)}, bf16[2,6,112,512]{3,2,1,0:T(8,128)(2,1)S(1)}, u32[]{:S(2)}, u32[]{:S(2)}) collective-permute-start(bf16[2,6,112,512]{3,2,1,0:T(8,128)(2,1)S(1)} %pad_maximum_fusion.3), channel_id=1, source_target_pairs={{0,31},{1,0},{2,1},{3,2},{4,3},{5,4},{6,5},{7,6},{8,7},{9,8},{10,9... | collective-permute-start | bytes 4128776 | tf_op jit(solution)/shard_map/ppermute | solution.py:31
  42.5 7.8 %copy-start.2 = (bf16[2048,512]{1,0:T(8,128)(2,1)S(1)}, bf16[2048,512]{1,0:T(8,128)(2,1)}, u32[]{:S(2)}) copy-start(bf16[2048,512]{1,0:T(8,128)(2,1)} %refs_18_.3) | copy-start | bytes 6291460
  42.5 7.8 %copy-start.7 = (f32[144,144]{1,0:T(8,128)S(1)}, f32[144,144]{1,0:T(8,128)}, u32[]{:S(2)}) copy-start(f32[144,144]{1,0:T(8,128)} %constant.34.clone.refs_10_) | copy-start | bytes 248836
  42.5 7.8 %copy-start.11 = (bf16[128,168]{1,0:T(8,128)(2,1)S(1)}, bf16[128,168]{1,0:T(8,128)(2,1)}, u32[]{:S(2)}) copy-start(bf16[128,168]{1,0:T(8,128)(2,1)} %constant.32.clone.refs_8_) | copy-start | bytes 129028
  42.5 7.8 %copy-start.12 = (bf16[128,144]{1,0:T(8,128)(2,1)S(1)}, bf16[128,144]{1,0:T(8,128)(2,1)}, u32[]{:S(2)}) copy-start(bf16[128,144]{1,0:T(8,128)(2,1)} %constant.31.clone.refs_7_) | copy-start | bytes 110596
  42.6 50.2 %collective-permute-start.2 = (bf16[2,6,112,512]{3,2,1,0:T(8,128)(2,1)S(1)}, bf16[2,6,112,512]{3,2,1,0:T(8,128)(2,1)S(1)}, u32[]{:S(2)}, u32[]{:S(2)}) collective-permute-start(bf16[2,6,112,512]{3,2,1,0:T(8,128)(2,1)S(1)} %pad_maximum_fusion), channel_id=1, source_target_pairs={{0,1},{1,2},{2,3},{3,4},{4,5},{5,6},{6,7},{7,8},{8,9},{9,10},{10,1... | collective-permute-start | bytes 4128776 | tf_op jit(solution)/shard_map/ppermute | solution.py:31
  42.7 7.6 %copy-start.1 = (bf16[512,2048]{1,0:T(8,128)(2,1)S(1)}, bf16[512,2048]{1,0:T(8,128)(2,1)}, u32[]{:S(2)}) copy-start(bf16[512,2048]{1,0:T(8,128)(2,1)} %refs_17_.3) | copy-start | bytes 6291460
  42.7 7.6 %copy-start.4 = (bf16[512,512]{1,0:T(8,128)(2,1)S(1)}, bf16[512,512]{1,0:T(8,128)(2,1)}, u32[]{:S(2)}) copy-start(bf16[512,512]{1,0:T(8,128)(2,1)} %refs_16_.3) | copy-start | bytes 1572868
  42.7 7.6 %copy-start.6 = (f32[512]{0:T(512)S(1)}, f32[512]{0:T(512)}, u32[]{:S(2)}) copy-start(f32[512]{0:T(512)} %param.20) | copy-start | bytes 6148
  42.7 7.6 %copy-start.10 = (bf16[128,144]{1,0:T(8,128)(2,1)S(1)}, bf16[128,144]{1,0:T(8,128)(2,1)}, u32[]{:S(2)}) copy-start(bf16[128,144]{1,0:T(8,128)(2,1)} %constant.33.clone.refs_9_) | copy-start | bytes 110596
  42.8 50.0 %collective-permute-start.3 = (bf16[2,6,112,512]{3,2,1,0:T(8,128)(2,1)S(1)}, bf16[2,6,112,512]{3,2,1,0:T(8,128)(2,1)S(1)}, u32[]{:S(2)}, u32[]{:S(2)}) collective-permute-start(bf16[2,6,112,512]{3,2,1,0:T(8,128)(2,1)S(1)} %pad_maximum_fusion.1), channel_id=1, source_target_pairs={{0,31},{1,0},{2,1},{3,2},{4,3},{5,4},{6,5},{7,6},{8,7},{9,8},{10,9... | collective-permute-start | bytes 4128776 | tf_op jit(solution)/shard_map/ppermute | solution.py:31
